TPU v7x, 128 devices: a whole 4x4x4 slice. The times are simulated.
128 devices in a mesh: wide: 64 (over z, y, x), narrow: 2 (over core).
Axes of the slice: x: 4, y: 4, z: 4, core: 2. Of those that a mesh axis runs over, the one named last changes fastest.
Arguments:
- cache: bfloat16 [512, 1024, 576], P('wide'), may hold values from -4 to 4
- lengths: int32 [512], P('wide'), may hold values from 0 to 1020, as said below
- mig_send: int32 [64, 2, 8], P('wide'), may hold values from 0 to 255, as said below
- mig_recv: int32 [64, 2, 8], P('wide'), may hold values from 0 to 255, as said below
- mig_count: int32 [64, 2], P('wide'), may hold values from 2 to 8, as said below
- queries: bfloat16 [4, 512, 128, 576], P(None, 'wide', 'narrow'), may hold values from -25 to 25
- new_latent: bfloat16 [4, 512, 576], P(None, 'wide'), may hold values from -4 to 4
- tokens: bfloat16 [4, 512, 7168], P(None, 'wide', 'narrow'), may hold values from -6 to 6
- expert_ids: int32 [4, 512, 8], P(None, 'wide'), may hold values from 0 to 31, all different within a row; in each aligned block of 8 rows (0 to 7, 8 to 15, ..., all dimensions but the last counted through in order) at most 4 rows name the same one
- affinity: float32 [4, 512, 8], P(None, 'wide'), may hold values from 0.05 to 1
- gate_weight: bfloat16 [7168, 32768], P('narrow', 'wide'), may hold values from -0.0625 to 0.0625
- up_weight: bfloat16 [7168, 32768], P('narrow', 'wide'), may hold values from -0.0625 to 0.0625
- down_weight: bfloat16 [32768, 7168], P('wide', 'narrow'), may hold values from -0.1875 to 0.1875
Outputs:
- context: bfloat16 [4, 512, 128, 512], P(None, 'wide', 'narrow')
- moe_out: bfloat16 [4, 512, 7168], P(None, 'wide', 'narrow')
Inputs may be any that keep to these rules, and one draw needn't show every extreme that they name: `lengths`: each rank sends one request to each of the two ranks after it; the slots that it sends from hold 0, the two slots that receive hold the arriving request's length, between 64 and 256, and every rank has a slot of length 1020. `mig_count`: entry [d, j] is the arriving request's length over 32 rounded up; one entry is 8 in every draw. `mig_send`: entry [s, j, k] is block k of the slot that rank s sends to rank s + j + 1; the two slots of a rank differ. `mig_recv`: entry [d, j, k] is block k of the slot of rank d that receives from rank d - j - 1; the two receiving slots of a rank differ from each other and from its sending slots. `expert_ids`: the 8 rows of one wide rank at one step name one expert at most 4 times.
All inputs are finite; a program needn't handle non-finite values.
Results may differ from a plain program's by a relative error of at most 0.0057.
Values may be sent and summed in bfloat16 or wider, within the bound.
No kernel may reach another device: no remote copies, remote signals or barrier semaphores. Data moves between devices by JAX's collectives and lax.ppermute only.
A program may use at most 128 MiB of HBM per device.

v0:
```python
import functools

import jax
import jax.numpy as jnp
from jax import lax
from jax.experimental import pallas as pl
from jax.experimental.pallas import tpu as pltpu
from jax.sharding import PartitionSpec as P

LAT = 512
STEPS = 4
MOST = 4
SIDE = 4
RANKS = SIDE * SIDE
MOVED = 256
TILE = 512
BATCHES = ((0, 1), (2, 3))
ORDERS = ((("x", "y", "z"), ("x", "z", "y")), (("y", "x", "z"), ("z", "x", "y")))
BACKS = ORDERS[::-1]
STRIDE = {"z": 16, "y": 4, "x": 1}
BOTH = ("wide", "narrow")
VMEM = 28 * 1024 * 1024

score_scale = 192.0 ** (-0.5)
route_scale = 2.5


def params(**more):
    return pltpu.CompilerParams(vmem_limit_bytes=VMEM, **more)


def moved_along(rank, axis, steps):
    place = rank // STRIDE[axis] % SIDE
    return rank + ((place + steps) % SIDE - place) * STRIDE[axis]


def hop(value, axes, steps):
    if steps == 0:
        return value
    pairs = [
        (rank * 2 + core, moved_along(rank, axes[core], steps) * 2 + core)
        for rank in range(64)
        for core in range(2)
    ]
    return lax.ppermute(value, BOTH, pairs)


def axes_at(orders, stage):
    return tuple(order[stage] for order in orders)


def attend_kernel(lengths, receivers, query_ref, cache_ref, moved_ref, fresh_ref, out_ref):
    slot = pl.program_id(0)
    length = lengths[slot]
    blocks = (length + 255) // 256
    steps, _, heads, width = query_ref.shape
    rows = steps * heads
    contract_last = (((1,), (1,)), ((), ()))

    def run(count):
        query = query_ref[...].reshape(rows, width)
        fresh = fresh_ref[0]
        fresh_scores = (
            lax.dot_general(query, fresh, contract_last, preferred_element_type=jnp.float32)
            * score_scale
        )
        row_step = lax.broadcasted_iota(jnp.int32, fresh_scores.shape, 0) // heads
        column = lax.broadcasted_iota(jnp.int32, fresh_scores.shape, 1)
        fresh_scores = jnp.where(column <= row_step, fresh_scores, -jnp.inf)
        peak = jnp.max(fresh_scores, axis=1, keepdims=True)
        keys = []
        scores = []
        for index in range(count):
            key = cache_ref[0, :, index * 256 : (index + 1) * 256]
            if count == 1:
                key = jnp.where(slot == receivers[0], moved_ref[0], key)
                key = jnp.where(slot == receivers[1], moved_ref[1], key)
            score = jnp.dot(query, key, preferred_element_type=jnp.float32) * score_scale
            if index == count - 1:
                position = lax.broadcasted_iota(jnp.int32, score.shape, 1) + index * 256
                score = jnp.where(position < length, score, -jnp.inf)
            peak = jnp.maximum(peak, jnp.max(score, axis=1, keepdims=True))
            keys.append(key)
            scores.append(score)
        fresh_exp = jnp.exp(fresh_scores - peak)
        total = jnp.sum(fresh_exp, axis=1, keepdims=True)
        exps = []
        for score in scores:
            weight = jnp.exp(score - peak)
            total = total + jnp.sum(weight, axis=1, keepdims=True)
            exps.append(weight)
        inverse = 1.0 / total
        context = jnp.dot(
            (fresh_exp * inverse).astype(jnp.bfloat16),
            fresh[:, :LAT],
            preferred_element_type=jnp.float32,
        )
        for weight, key in zip(exps, keys):
            context = context + lax.dot_general(
                (weight * inverse).astype(jnp.bfloat16),
                key[:LAT],
                contract_last,
                preferred_element_type=jnp.float32,
            )
        out_ref[...] = context.astype(jnp.bfloat16).reshape(out_ref.shape)

    for count in range(5):
        pl.when(blocks == count)(functools.partial(run, count))


def attend(queries, cache, lengths, receivers, moved, new_latent):
    steps, slots, heads, width = queries.shape
    fresh = jnp.pad(jnp.swapaxes(new_latent, 0, 1), ((0, 0), (0, 16 - steps), (0, 0)))
    return pl.pallas_call(
        attend_kernel,
        grid_spec=pltpu.PrefetchScalarGridSpec(
            num_scalar_prefetch=2,
            grid=(slots,),
            in_specs=[
                pl.BlockSpec((steps, 1, heads, width), lambda i, *_: (0, i, 0, 0)),
                pl.BlockSpec((1, width, cache.shape[2]), lambda i, *_: (i, 0, 0)),
                pl.BlockSpec(moved.shape, lambda i, *_: (0, 0, 0)),
                pl.BlockSpec((1, 16, width), lambda i, *_: (i, 0, 0)),
            ],
            out_specs=pl.BlockSpec((steps, 1, heads, LAT), lambda i, *_: (0, i, 0, 0)),
        ),
        out_shape=jax.ShapeDtypeStruct((steps, slots, heads, LAT), jnp.bfloat16),
        compiler_params=params(),
        cost_estimate=pl.CostEstimate(
            flops=2 * 18 * 256 * 256 * 1280, bytes_accessed=14_000_000, transcendentals=18 * 256 * 256
        ),
        name="attend",
    )(lengths, receivers, queries, cache, moved, fresh)


def pack_kernel(token_ref, id_ref, affinity_ref, *out_refs):
    steps, requests, half_width = token_ref.shape
    topk = id_ref.shape[2]
    rows = steps * requests
    ids = id_ref[...].reshape(rows, topk)
    affinity = affinity_ref[...].reshape(rows, topk)
    share = route_scale * affinity / jnp.sum(affinity, axis=1, keepdims=True)
    high = share.astype(jnp.bfloat16).astype(jnp.float32)
    low = share - high
    lane = lax.broadcasted_iota(jnp.int32, (rows, 128), 1)
    hot = jnp.zeros((rows, 128), jnp.float32)
    shares = jnp.zeros((rows, 128), jnp.float32)
    for k in range(topk):
        named = ids[:, k : k + 1]
        hot = jnp.where(lane == named, 1.0, hot)
        shares = jnp.where(lane == named + 32, high[:, k : k + 1], shares)
        shares = jnp.where(lane == named + 64, low[:, k : k + 1], shares)
    row = lax.broadcasted_iota(jnp.int32, (rows, rows), 0)
    other = lax.broadcasted_iota(jnp.int32, (rows, rows), 1)
    earlier = ((other < row) & (row // requests == other // requests)).astype(jnp.bfloat16)
    before = jnp.dot(earlier, hot.astype(jnp.bfloat16), preferred_element_type=jnp.float32)
    routing = jnp.where(lane < 32, jnp.where(hot > 0.5, before, -1.0), shares).astype(jnp.bfloat16)
    features = token_ref[...].reshape(rows, half_width)
    start = 0
    for out_ref in out_refs:
        count = out_ref.shape[0]
        out_ref[:, :half_width] = features[start : start + count]
        out_ref[:, half_width:] = routing[start : start + count]
        start += count


def pack(tokens, expert_ids, affinity):
    steps, requests, half_width = tokens.shape
    return pl.pallas_call(
        pack_kernel,
        out_shape=[
            jax.ShapeDtypeStruct((len(batch) * requests, half_width + 128), jnp.bfloat16) for batch in BATCHES
        ],
        name="pack",
    )(tokens, expert_ids, affinity)


def along_lanes(aux, wanted, shape, transposed):
    if transposed:
        lane = lax.broadcasted_iota(jnp.int32, (shape[0], 128), 1)
        chosen = (lane == wanted).astype(jnp.bfloat16)
        return lax.dot_general(
            chosen, aux, (((1,), (1,)), ((), ())), preferred_element_type=jnp.float32
        )
    lane = lax.broadcasted_iota(jnp.int32, (128, shape[1]), 0)
    chosen = (lane == wanted).astype(jnp.bfloat16)
    return jnp.dot(aux, chosen, preferred_element_type=jnp.float32)


def placed(aux, expert, shape, transposed):
    place = along_lanes(aux, expert, shape, transposed).astype(jnp.int32)
    row = lax.broadcasted_iota(jnp.int32, shape, 1 if transposed else 0)
    cell = lax.broadcasted_iota(jnp.int32, shape, 0 if transposed else 1)
    return (place >= 0) & (row // 8 * MOST + place == cell)


def pick_kernel(experts, *refs):
    piece_refs, out_refs = refs[:4], refs[4:8]
    cells, half_width = out_refs[0].shape
    aux = jnp.concatenate([ref[:, half_width:] for ref in piece_refs], axis=0)
    pickers = [
        placed(aux, experts[index], (cells, aux.shape[0]), True).astype(jnp.bfloat16)
        for index in range(SIDE)
    ]
    for start in range(0, half_width, TILE):
        rows = jnp.concatenate([ref[:, start : start + TILE] for ref in piece_refs], axis=0)
        for index in range(SIDE):
            out_refs[index][:, start : start + TILE] = jnp.dot(
                pickers[index], rows, preferred_element_type=jnp.float32
            ).astype(jnp.bfloat16)


IN_SMEM = pl.BlockSpec(memory_space=pltpu.SMEM)
IN_VMEM = pl.BlockSpec(memory_space=pltpu.VMEM)


def pick(experts, pieces, half_width):
    rows = pieces[0].shape[0] * SIDE
    cells = rows // 2
    return pl.pallas_call(
        pick_kernel,
        in_specs=[IN_SMEM] + [IN_VMEM] * SIDE,
        out_specs=[IN_VMEM] * SIDE,
        out_shape=[jax.ShapeDtypeStruct((cells, half_width), jnp.bfloat16)] * SIDE,
        compiler_params=params(),
        cost_estimate=pl.CostEstimate(
            flops=2 * SIDE * cells * rows * half_width,
            bytes_accessed=2 * (SIDE * cells + rows) * half_width,
            transcendentals=0,
        ),
        name="pick",
    )(experts, *pieces)


def mix_kernel(by_inner, experts, *refs):
    piece_refs, cell_refs, out_refs = refs[:4], refs[4:8], refs[8:12]
    cells, half_width = cell_refs[0].shape
    rows_each = out_refs[0].shape[0]
    rows = rows_each * SIDE
    each = rows_each // SIDE
    aux = jnp.concatenate([ref[:, half_width:] for ref in piece_refs], axis=0)
    mixers = []
    for index in range(SIDE):
        chosen = placed(aux, experts[index], (rows, cells), False)
        for part in range(2):
            share = along_lanes(aux, experts[index] + 32 * (part + 1), (rows, cells), False)
            mixers.append(jnp.where(chosen, share, 0.0).astype(jnp.bfloat16))
    high = jnp.concatenate(mixers[0::2], axis=1)
    low = jnp.concatenate(mixers[1::2], axis=1)
    for start in range(0, half_width, TILE):
        answers = jnp.concatenate([ref[:, start : start + TILE] for ref in cell_refs], axis=0)
        mixed = jnp.dot(high, answers, preferred_element_type=jnp.float32)
        mixed = mixed + jnp.dot(low, answers, preferred_element_type=jnp.float32)
        mixed = mixed.astype(jnp.bfloat16)
        for outer in range(SIDE):
            for inner in range(SIDE):
                block = mixed[(outer * SIDE + inner) * each : (outer * SIDE + inner + 1) * each]
                piece, place = (inner, outer) if by_inner else (outer, inner)
                out_refs[piece][place * each : (place + 1) * each, start : start + TILE] = block


def mix(experts, pieces, answers, by_inner):
    rows_each = pieces[0].shape[0]
    rows = rows_each * SIDE
    cells, half_width = answers[0].shape
    return pl.pallas_call(
        functools.partial(mix_kernel, by_inner),
        in_specs=[IN_SMEM] + [IN_VMEM] * 2 * SIDE,
        out_specs=[IN_VMEM] * SIDE,
        out_shape=[jax.ShapeDtypeStruct((rows_each, half_width), jnp.bfloat16)] * SIDE,
        compiler_params=params(),
        cost_estimate=pl.CostEstimate(
            flops=2 * 2 * SIDE * cells * rows * half_width,
            bytes_accessed=2 * (SIDE * cells + rows) * half_width,
            transcendentals=0,
        ),
        name="mix",
    )(experts, *pieces, *answers)


def widen_kernel(strides, *refs):
    row_refs, gate_ref, up_ref, out_gate, out_up = refs[:4], *refs[4:]
    cells = row_refs[0].shape[0]
    each = cells // RANKS
    units = gate_ref.shape[1]
    rows = jnp.concatenate([ref[...] for ref in row_refs], axis=0)
    for weight_ref, out_ref in ((gate_ref, out_gate), (up_ref, out_up)):
        for start in range(0, units, 256):
            part = jnp.dot(
                rows, weight_ref[:, start : start + 256], preferred_element_type=jnp.float32
            )
            for outer in range(SIDE):
                for middle in range(SIDE):
                    for inner in range(SIDE):
                        block = (outer * SIDE + middle) * SIDE + inner
                        place = outer * strides[0] + middle * strides[1] + inner * strides[2]
                        place = pl.multiple_of(place * each, each)
                        out_ref[pl.ds(place, each), start : start + 256] = part[
                            block * each : (block + 1) * each
                        ]


def widen(strides, rows, gate_weight, up_weight):
    cells, half_width = rows[0].shape
    units = gate_weight.shape[1]
    total = SIDE * cells
    return pl.pallas_call(
        widen_kernel,
        in_specs=[IN_SMEM] + [IN_VMEM] * (SIDE + 2),
        out_specs=[IN_VMEM] * 2,
        out_shape=[jax.ShapeDtypeStruct((total, units), jnp.float32)] * 2,
        compiler_params=params(),
        cost_estimate=pl.CostEstimate(
            flops=4 * total * half_width * units,
            bytes_accessed=2 * (total + 2 * units) * half_width + 8 * total * units,
            transcendentals=0,
        ),
        name="widen",
    )(strides, *rows, gate_weight, up_weight)


def narrow_kernel(strides, *refs):
    gate_own, gate_other, up_own, up_other, weight_ref = refs[:5]
    out_refs, hidden = refs[5:9], refs[9]
    cells, half_width = out_refs[0].shape
    each = cells // RANKS
    for outer in range(SIDE):
        for middle in range(SIDE):
            parts = []
            for inner in range(SIDE):
                place = outer * strides[0] + middle * strides[1] + inner * strides[2]
                place = pl.ds(pl.multiple_of(place * each, each), each)
                gate = gate_own[place, :] + gate_other[place, :]
                up = up_own[place, :] + up_other[place, :]
                parts.append(gate / (1.0 + jnp.exp(-gate)) * up)
            block = (outer * SIDE + middle) * SIDE
            hidden[block * each : (block + SIDE) * each, :] = jnp.concatenate(
                parts, axis=0
            ).astype(jnp.bfloat16)
    for start in range(0, half_width, TILE):
        result = jnp.dot(
            hidden[...], weight_ref[:, start : start + TILE], preferred_element_type=jnp.float32
        )
        for index in range(SIDE):
            out_refs[index][:, start : start + TILE] = result[
                index * cells : (index + 1) * cells
            ].astype(jnp.bfloat16)


def narrow(strides, gate_own, gate_other, up_own, up_other, down_weight):
    total, units = gate_own.shape
    cells = total // SIDE
    half_width = down_weight.shape[1]
    return pl.pallas_call(
        narrow_kernel,
        in_specs=[IN_SMEM] + [IN_VMEM] * 5,
        out_specs=[IN_VMEM] * SIDE,
        out_shape=[jax.ShapeDtypeStruct((cells, half_width), jnp.bfloat16)] * SIDE,
        scratch_shapes=[pltpu.VMEM((total, units), jnp.bfloat16)],
        compiler_params=params(),
        cost_estimate=pl.CostEstimate(
            flops=2 * total * half_width * units,
            bytes_accessed=2 * (total + units) * half_width + 16 * total * units,
            transcendentals=total * units,
        ),
        name="narrow",
    )(strides, gate_own, gate_other, up_own, up_other, down_weight)


def swap_cores(value):
    return lax.ppermute(value, "narrow", [(0, 1), (1, 0)])


def add_up(values):
    total = values[0].astype(jnp.float32)
    for value in values[1:]:
        total = total + value.astype(jnp.float32)
    return total.astype(jnp.bfloat16)


def body(
    cache,
    lengths,
    mig_send,
    mig_recv,
    mig_count,
    queries,
    new_latent,
    tokens,
    expert_ids,
    affinity,
    gate_weight,
    up_weight,
    down_weight,
):
    core = lax.axis_index("narrow")
    rank = lax.axis_index("wide")
    slot_count, capacity, width = cache.shape
    per_slot = capacity // 32
    requests, half_width = tokens.shape[1:]

    keys_last = jnp.swapaxes(cache, 1, 2)
    sending = mig_send[0, core, 0] // per_slot
    outgoing = lax.dynamic_slice(keys_last, (sending, 0, 0), (1, width, MOVED))[0]
    pairs = [(r * 2 + j, (r + j + 1) % 64 * 2 + j) for r in range(64) for j in range(2)]
    arrived = lax.ppermute(outgoing, BOTH, pairs)
    arrived_other = swap_cores(arrived)
    receivers = jnp.stack([mig_recv[0, core, 0], mig_recv[0, 1 - core, 0]]) // per_slot
    moved = jnp.stack([arrived, arrived_other])

    reach = []
    for steps in range(SIDE):
        by_core = [moved_along(rank, ORDERS[0][c][2], steps) // 2 for c in range(2)]
        reach.append(jnp.where(core == 0, by_core[0], by_core[1]))
    experts = jnp.stack(reach).astype(jnp.int32)
    scale = {"z": 16, "y": 4, "x": 1}

    own_rows = pack(tokens, expert_ids, affinity)
    gathered = []
    for index in range(len(BATCHES)):
        orders = ORDERS[index]
        first = [hop(own_rows[index], axes_at(orders, 0), steps) for steps in range(SIDE)]
        plane_row = jnp.concatenate(first, axis=0)
        gathered.append([hop(plane_row, axes_at(orders, 1), steps) for steps in range(SIDE)])
    picked = []
    for index in range(len(BATCHES)):
        if index == 1:
            context = attend(queries, keys_last, lengths, receivers, moved, new_latent)
            gathered[1], context = lax.optimization_barrier((gathered[1], context))
        rows = pick(experts, gathered[index], half_width)
        picked.append([hop(rows[steps], axes_at(ORDERS[index], 2), steps) for steps in range(SIDE)])

    outputs = []
    for index, (pieces, rows) in enumerate(zip(gathered, picked)):
        orders, backs = ORDERS[index], BACKS[index]
        by_core = [[scale[axis] for axis in order[::-1]] for order in orders]
        strides = jnp.where(
            core == 0, jnp.array(by_core[0], jnp.int32), jnp.array(by_core[1], jnp.int32)
        )
        gate, up = widen(strides, rows, gate_weight, up_weight)
        answers = narrow(strides, gate, swap_cores(gate), up, swap_cores(up), down_weight)
        answers = [hop(answers[steps], axes_at(orders, 2), -steps) for steps in range(SIDE)]
        mixed = mix(experts, pieces, answers, backs[0][1] == orders[0][0])
        mixed = add_up([hop(mixed[steps], axes_at(backs, 1), -steps) for steps in range(SIDE)])
        mixed = mixed.reshape(SIDE, -1, half_width)
        outputs.append(
            add_up([hop(mixed[steps], axes_at(backs, 0), -steps) for steps in range(SIDE)])
        )
    moe_out = jnp.concatenate(outputs, axis=0).reshape(STEPS, requests, half_width)
    return (context, moe_out)


def solution(mesh):
    specs = (
        P("wide", None, None),
        P("wide"),
        P("wide", None, None),
        P("wide", None, None),
        P("wide", None),
        P(None, "wide", "narrow", None),
        P(None, "wide", None),
        P(None, "wide", "narrow"),
        P(None, "wide", None),
        P(None, "wide", None),
        P("narrow", "wide"),
        P("narrow", "wide"),
        P("wide", "narrow"),
    )
    return jax.shard_map(
        body,
        mesh=mesh,
        in_specs=specs,
        out_specs=(P(None, "wide", "narrow", None), P(None, "wide", "narrow")),
        check_vma=False,
    )
```

profile of v0, /device:TPU:0, one launch (start us, length us, event | category | flops | bytes accessed | tf_op | source)
XLA Modules:
  0.0 188.5 jit_solution(11575031663402138363)
XLA Ops:
  0.6 2.0 %pack.1 = (bf16[16,3712]{1,0:T(8,128)(2,1)}, bf16[16,3712]{1,0:T(8,128)(2,1)}) custom-call(bf16[4,8,3584]{2,1,0:T(8,128)(2,1)} %token_ref.1, s32[4,8,8]{2,1,0:T(8,128)} %id_ref.1, f32[4,8,8]{2,1,0:T(8,128)} %affinity_ref.1), custom_call_target="tpu_custom_call" | custom-call | tf_op jit(solution)/shard_map/pack/pallas_call | solution.py:169
  4.2 2.7 %collective-permute-start.9 = (bf16[16,3712]{1,0:T(8,128)(2,1)}, bf16[16,3712]{1,0:T(8,128)(2,1)}, u32[]{:S(2)}, u32[]{:S(2)}) collective-permute-start(bf16[16,3712]{1,0:T(8,128)(2,1)} %get-tuple-element.39), channel_id=1, source_target_pairs={{0,4},{1,5},{2,6},{3,7},{4,0},{5,1},{6,2},{7,3},{8,12},{9,13},{10,... | collective-permute-start | bytes 356360 | tf_op jit(solution)/shard_map/ppermute | solution.py:45
  10.0 2.9 %collective-permute-start.1 = (bf16[16,3712]{1,0:T(8,128)(2,1)}, bf16[16,3712]{1,0:T(8,128)(2,1)S(1)}, u32[]{:S(2)}, u32[]{:S(2)}) collective-permute-start(bf16[16,3712]{1,0:T(8,128)(2,1)} %get-tuple-element.37), channel_id=1, source_target_pairs={{0,16},{1,65},{2,18},{3,67},{4,20},{5,69},{6,22},{7,71},{8,24},{9,... | collective-permute-start | bytes 356360 | tf_op jit(solution)/shard_map/ppermute | solution.py:45
  27.6 1.9 %collective-permute-start.13 = (bf16[64,3712]{1,0:T(8,128)(2,1)}, bf16[64,3712]{1,0:T(8,128)(2,1)S(1)}, u32[]{:S(2)}, u32[]{:S(2)}) collective-permute-start(bf16[64,3712]{1,0:T(8,128)(2,1)} %constant_dynamic-update-slice_fusion.4.refs_0_), channel_id=1, source_target_pairs={{0,24},{1,97},{2,26},{3,99},{4,28},{5,101},{6,30},{7,103},{8,0},{9... | collective-permute-start | bytes 1425416 | tf_op jit(solution)/shard_map/ppermute | solution.py:45
  29.8 15.7 %collective-permute-done.11.refs_1_ = bf16[64,3712]{1,0:T(8,128)(2,1)S(1)} collective-permute-done((bf16[64,3712]{1,0:T(8,128)(2,1)}, bf16[64,3712]{1,0:T(8,128)(2,1)S(1)}, u32[]{:S(2)}, u32[]{:S(2)}) %collective-permute-start.11) | collective-permute-done | bytes 475168 | tf_op jit(solution)/shard_map/ppermute | solution.py:45
  46.9 1.9 pick.2
  48.7 2.0 %collective-permute-start.14 = (bf16[128,3584]{1,0:T(8,128)(2,1)S(1)}, bf16[128,3584]{1,0:T(8,128)(2,1)S(1)}, u32[]{:S(2)}, u32[]{:S(2)}) collective-permute-start(bf16[128,3584]{1,0:T(8,128)(2,1)S(1)} %get-tuple-element.41), channel_id=1, source_target_pairs={{0,32},{1,9},{2,34},{3,11},{4,36},{5,13},{6,38},{7,15},{8,40},{9,1... | collective-permute-start | bytes 2752520 | tf_op jit(solution)/shard_map/ppermute | solution.py:45
  50.7 2.6 %collective-permute-start.15 = (bf16[128,3584]{1,0:T(8,128)(2,1)S(1)}, bf16[128,3584]{1,0:T(8,128)(2,1)S(1)}, u32[]{:S(2)}, u32[]{:S(2)}) collective-permute-start(bf16[128,3584]{1,0:T(8,128)(2,1)S(1)} %get-tuple-element.42), channel_id=1, source_target_pairs={{0,64},{1,17},{2,66},{3,19},{4,68},{5,21},{6,70},{7,23},{8,72},{9,... | collective-permute-start | bytes 2752520 | tf_op jit(solution)/shard_map/ppermute | solution.py:45
  57.5 3.7 %copy-done.1 = bf16[8,1024,576]{1,2,0:T(8,128)(2,1)S(1)} copy-done((bf16[8,1024,576]{1,2,0:T(8,128)(2,1)S(1)}, bf16[8,1024,576]{1,2,0:T(8,128)(2,1)}, u32[]{:S(2)}) %copy-start.1) | copy-done | bytes 9437208
  61.2 12.4 %attend.1 = bf16[4,8,64,512]{3,2,1,0:T(8,128)(2,1)} custom-call(s32[8]{0:T(128)S(1)} %copy-done.5, s32[2]{0:T(128)S(1)} %and_select_fusion.receivers, bf16[4,8,64,576]{3,2,1,0:T(8,128)(2,1)S(1)} %copy-done.2, bf16[8,576,1024]{2,1,0:T(8,128)(2,1)S(1)} %bitcast.19, bf16[2,576,256]{2,1,0:T(8,128)(2,1)S(1)} %pad_maximum_fusion.moved_ref, ...), custom_call_target="tpu_custom_call" | custom-call | flops 3019898880 | bytes 14000000 | tf_op jit(solution)/shard_map/attend/pallas_call | solution.py:114
  80.4 2.5 %collective-permute-start.30 = (bf16[128,3584]{1,0:T(8,128)(2,1)S(1)}, bf16[128,3584]{1,0:T(8,128)(2,1)S(1)}, u32[]{:S(2)}, u32[]{:S(2)}) collective-permute-start(bf16[128,3584]{1,0:T(8,128)(2,1)S(1)} %get-tuple-element.61), channel_id=1, source_target_pairs={{0,96},{1,25},{2,98},{3,27},{4,100},{5,29},{6,102},{7,31},{8,104},... | collective-permute-start | bytes 2752520 | tf_op jit(solution)/shard_map/ppermute | solution.py:45
  83.0 4.6 %widen.2 = (f32[512,512]{1,0:T(8,128)S(1)}, f32[512,512]{1,0:T(8,128)S(1)}) custom-call(s32[3]{0:T(128)S(1)} %broadcast_select_fusion.1.strides, bf16[128,3584]{1,0:T(8,128)(2,1)S(1)} %get-tuple-element.40.refs_0_, bf16[128,3584]{1,0:T(8,128)(2,1)S(1)} %collective-permute-done.14.refs_1_, bf16[128,3584]{1,0:T(8,128)(2,1)S(1)} %collective-permute-done.15.refs_2_, ...), custom_call_target="tpu_custom_call" | custom-call | flops 3758096384 | bytes 13107200 | tf_op jit(solution)/shard_map/widen/pallas_call | solution.py:307
  88.2 13.6 %collective-permute-done.28.refs_1_ = bf16[128,3584]{1,0:T(8,128)(2,1)S(1)} collective-permute-done((bf16[128,3584]{1,0:T(8,128)(2,1)S(1)}, bf16[128,3584]{1,0:T(8,128)(2,1)S(1)}, u32[]{:S(2)}, u32[]{:S(2)}) %collective-permute-start.28) | collective-permute-done | bytes 917536 | tf_op jit(solution)/shard_map/ppermute | solution.py:45
  102.7 4.6 %widen.3 = (f32[512,512]{1,0:T(8,128)S(1)}, f32[512,512]{1,0:T(8,128)S(1)}) custom-call(s32[3]{0:T(128)S(1)} %broadcast_select_fusion.strides, bf16[128,3584]{1,0:T(8,128)(2,1)S(1)} %get-tuple-element.58.refs_0_, bf16[128,3584]{1,0:T(8,128)(2,1)S(1)} %collective-permute-done.28.refs_1_, bf16[128,3584]{1,0:T(8,128)(2,1)S(1)} %collective-permute-done.29.refs_2_, ...), custom_call_target="tpu_custom_call" | custom-call | flops 3758096384 | bytes 13107200 | tf_op jit(solution)/shard_map/widen/pallas_call | solution.py:307
  107.9 2.7 %narrow.2 = (bf16[128,3584]{1,0:T(8,128)(2,1)S(1)}, bf16[128,3584]{1,0:T(8,128)(2,1)S(1)}, bf16[128,3584]{1,0:T(8,128)(2,1)S(1)}, bf16[128,3584]{1,0:T(8,128)(2,1)S(1)}) custom-call(s32[3]{0:T(128)S(1)} %broadcast_select_fusion.1.strides, f32[512,512]{1,0:T(8,128)S(1)} %get-tuple-element.44.refs_0_, f32[512,512]{1,0:T(8,128)S(1)} %collective-permute-done.17.refs_1_, ...), custom_call_target="tpu_custom_call" | custom-call | flops 1879048192 | bytes 11534336 | tf_op jit(solution)/shard_map/narrow/pallas_call | solution.py:354
  110.6 2.7 %collective-permute-start.19 = (bf16[128,3584]{1,0:T(8,128)(2,1)S(1)}, bf16[128,3584]{1,0:T(8,128)(2,1)S(1)}, u32[]{:S(2)}, u32[]{:S(2)}) collective-permute-start(bf16[128,3584]{1,0:T(8,128)(2,1)S(1)} %get-tuple-element.47), channel_id=1, source_target_pairs={{0,96},{1,25},{2,98},{3,27},{4,100},{5,29},{6,102},{7,31},{8,104},... | collective-permute-start | bytes 2752520 | tf_op jit(solution)/shard_map/ppermute | solution.py:45
  115.1 2.7 %narrow.3 = (bf16[128,3584]{1,0:T(8,128)(2,1)S(1)}, bf16[128,3584]{1,0:T(8,128)(2,1)S(1)}, bf16[128,3584]{1,0:T(8,128)(2,1)S(1)}, bf16[128,3584]{1,0:T(8,128)(2,1)S(1)}) custom-call(s32[3]{0:T(128)S(1)} %broadcast_select_fusion.strides, f32[512,512]{1,0:T(8,128)S(1)} %get-tuple-element.62.refs_0_, f32[512,512]{1,0:T(8,128)S(1)} %collective-permute-done.31.refs_1_, ...), custom_call_target="tpu_custom_call" | custom-call | flops 1879048192 | bytes 11534336 | tf_op jit(solution)/shard_map/narrow/pallas_call | solution.py:354
  117.9 3.0 %collective-permute-start.33 = (bf16[128,3584]{1,0:T(8,128)(2,1)S(1)}, bf16[128,3584]{1,0:T(8,128)(2,1)S(1)}, u32[]{:S(2)}, u32[]{:S(2)}) collective-permute-start(bf16[128,3584]{1,0:T(8,128)(2,1)S(1)} %get-tuple-element.65), channel_id=1, source_target_pairs={{0,96},{1,25},{2,98},{3,27},{4,100},{5,29},{6,102},{7,31},{8,104},... | collective-permute-start | bytes 2752520 | tf_op jit(solution)/shard_map/ppermute | solution.py:45
  121.8 12.3 %collective-permute-done.19.refs_5_ = bf16[128,3584]{1,0:T(8,128)(2,1)S(1)} collective-permute-done((bf16[128,3584]{1,0:T(8,128)(2,1)S(1)}, bf16[128,3584]{1,0:T(8,128)(2,1)S(1)}, u32[]{:S(2)}, u32[]{:S(2)}) %collective-permute-start.19) | collective-permute-done | bytes 917536 | tf_op jit(solution)/shard_map/ppermute | solution.py:45
  134.1 3.9 %collective-permute-done.21.refs_7_ = bf16[128,3584]{1,0:T(8,128)(2,1)S(1)} collective-permute-done((bf16[128,3584]{1,0:T(8,128)(2,1)S(1)}, bf16[128,3584]{1,0:T(8,128)(2,1)S(1)}, u32[]{:S(2)}, u32[]{:S(2)}) %collective-permute-start.21) | collective-permute-done | bytes 917536 | tf_op jit(solution)/shard_map/ppermute | solution.py:45
  138.1 2.9 %mix.2 = (bf16[64,3584]{1,0:T(8,128)(2,1)S(1)}, bf16[64,3584]{1,0:T(8,128)(2,1)S(1)}, bf16[64,3584]{1,0:T(8,128)(2,1)S(1)}, bf16[64,3584]{1,0:T(8,128)(2,1)S(1)}) custom-call(s32[4]{0:T(128)S(1)} %pad_add_fusion.1.experts, bf16[64,3712]{1,0:T(8,128)(2,1)S(1)} %copy-done.4, bf16[64,3712]{1,0:T(8,128)(2,1)S(1)} %copy-done.9, bf16[64,3712]{1,0:T(8,128)(2,1)S(1)} %copy-done.11, ...), custom_call_target="tpu_custom_call" | custom-call | flops 1879048192 | bytes 5505024 | tf_op jit(solution)/shard_map/mix/pallas_call | solution.py:266
  141.0 2.7 %collective-permute-start.22 = (bf16[64,3584]{1,0:T(8,128)(2,1)S(1)}, bf16[64,3584]{1,0:T(8,128)(2,1)S(1)}, u32[]{:S(2)}, u32[]{:S(2)}) collective-permute-start(bf16[64,3584]{1,0:T(8,128)(2,1)S(1)} %get-tuple-element.51), channel_id=1, source_target_pairs={{0,6},{1,7},{2,0},{3,1},{4,2},{5,3},{6,4},{7,5},{8,14},{9,15},{10,... | collective-permute-start | bytes 1376264 | tf_op jit(solution)/shard_map/ppermute | solution.py:45
  143.6 10.1 %collective-permute-done.33.refs_5_ = bf16[128,3584]{1,0:T(8,128)(2,1)S(1)} collective-permute-done((bf16[128,3584]{1,0:T(8,128)(2,1)S(1)}, bf16[128,3584]{1,0:T(8,128)(2,1)S(1)}, u32[]{:S(2)}, u32[]{:S(2)}) %collective-permute-start.33) | collective-permute-done | bytes 917536 | tf_op jit(solution)/shard_map/ppermute | solution.py:45
  154.0 3.8 %collective-permute-done.35.refs_7_ = bf16[128,3584]{1,0:T(8,128)(2,1)S(1)} collective-permute-done((bf16[128,3584]{1,0:T(8,128)(2,1)S(1)}, bf16[128,3584]{1,0:T(8,128)(2,1)S(1)}, u32[]{:S(2)}, u32[]{:S(2)}) %collective-permute-start.35) | collective-permute-done | bytes 917536 | tf_op jit(solution)/shard_map/ppermute | solution.py:45
  157.8 2.9 %mix.3 = (bf16[64,3584]{1,0:T(8,128)(2,1)S(1)}, bf16[64,3584]{1,0:T(8,128)(2,1)S(1)}, bf16[64,3584]{1,0:T(8,128)(2,1)S(1)}, bf16[64,3584]{1,0:T(8,128)(2,1)S(1)}) custom-call(s32[4]{0:T(128)S(1)} %pad_add_fusion.1.experts, bf16[64,3712]{1,0:T(8,128)(2,1)S(1)} %constant_dynamic-update-slice_fusion.refs_0_, ...), custom_call_target="tpu_custom_call" | custom-call | flops 1879048192 | bytes 5505024 | tf_op jit(solution)/shard_map/mix/pallas_call | solution.py:266
  160.7 2.0 %collective-permute-start.36 = (bf16[64,3584]{1,0:T(8,128)(2,1)S(1)}, bf16[64,3584]{1,0:T(8,128)(2,1)S(1)}, u32[]{:S(2)}, u32[]{:S(2)}) collective-permute-start(bf16[64,3584]{1,0:T(8,128)(2,1)S(1)} %get-tuple-element.69), channel_id=1, source_target_pairs={{0,24},{1,97},{2,26},{3,99},{4,28},{5,101},{6,30},{7,103},{8,0},{9... | collective-permute-start | bytes 1376264 | tf_op jit(solution)/shard_map/ppermute | solution.py:45
  166.2 3.8 %collective-permute-start.25 = (bf16[16,3584]{1,0:T(8,128)(2,1)S(1)}, bf16[16,3584]{1,0:T(8,128)(2,1)S(1)}, u32[]{:S(2)}, u32[]{:S(2)}) collective-permute-start(bf16[16,3584]{1,0:T(8,128)(2,1)S(1)} %get-tuple-element.72), channel_id=1, source_target_pairs={{0,24},{1,97},{2,26},{3,99},{4,28},{5,101},{6,30},{7,103},{8,0},{9... | collective-permute-start | bytes 344072 | tf_op jit(solution)/shard_map/ppermute | solution.py:45
  169.9 3.7 %collective-permute-done.36 = bf16[64,3584]{1,0:T(8,128)(2,1)S(1)} collective-permute-done((bf16[64,3584]{1,0:T(8,128)(2,1)S(1)}, bf16[64,3584]{1,0:T(8,128)(2,1)S(1)}, u32[]{:S(2)}, u32[]{:S(2)}) %collective-permute-start.36) | collective-permute-done | bytes 458784 | tf_op jit(solution)/shard_map/ppermute | solution.py:45
  173.6 3.9 %collective-permute-done.38 = bf16[64,3584]{1,0:T(8,128)(2,1)S(1)} collective-permute-done((bf16[64,3584]{1,0:T(8,128)(2,1)S(1)}, bf16[64,3584]{1,0:T(8,128)(2,1)S(1)}, u32[]{:S(2)}, u32[]{:S(2)}) %collective-permute-start.38) | collective-permute-done | bytes 458784 | tf_op jit(solution)/shard_map/ppermute | solution.py:45
  177.8 2.7 %collective-permute-start.39 = (bf16[16,3584]{1,0:T(8,128)(2,1)S(1)}, bf16[16,3584]{1,0:T(8,128)(2,1)S(1)}, u32[]{:S(2)}, u32[]{:S(2)}) collective-permute-start(bf16[16,3584]{1,0:T(8,128)(2,1)S(1)} %get-tuple-element.75), channel_id=1, source_target_pairs={{0,6},{1,7},{2,0},{3,1},{4,2},{5,3},{6,4},{7,5},{8,14},{9,15},{10,... | collective-permute-start | bytes 344072 | tf_op jit(solution)/shard_map/ppermute | solution.py:45
  181.5 2.5 %collective-permute-done.39 = bf16[16,3584]{1,0:T(8,128)(2,1)S(1)} collective-permute-done((bf16[16,3584]{1,0:T(8,128)(2,1)S(1)}, bf16[16,3584]{1,0:T(8,128)(2,1)S(1)}, u32[]{:S(2)}, u32[]{:S(2)}) %collective-permute-start.39) | collective-permute-done | bytes 114720 | tf_op jit(solution)/shard_map/ppermute | solution.py:45
  184.0 2.8 %collective-permute-done.40 = bf16[16,3584]{1,0:T(8,128)(2,1)S(1)} collective-permute-done((bf16[16,3584]{1,0:T(8,128)(2,1)S(1)}, bf16[16,3584]{1,0:T(8,128)(2,1)S(1)}, u32[]{:S(2)}, u32[]{:S(2)}) %collective-permute-start.40) | collective-permute-done | bytes 114720 | tf_op jit(solution)/shard_map/ppermute | solution.py:45
  (132 shorter events, 40.6 us)
Async XLA Ops:
  2.6 17.7 %collective-permute-start.8 = (bf16[16,3712]{1,0:T(8,128)(2,1)}, bf16[16,3712]{1,0:T(8,128)(2,1)}, u32[]{:S(2)}, u32[]{:S(2)}) collective-permute-start(bf16[16,3712]{1,0:T(8,128)(2,1)} %get-tuple-element.39), channel_id=1, source_target_pairs={{0,2},{1,3},{2,4},{3,5},{4,6},{5,7},{6,0},{7,1},{8,10},{9,11},{10,... | collective-permute-start | bytes 356360 | tf_op jit(solution)/shard_map/ppermute | solution.py:45
  4.2 19.1 %collective-permute-start.9 = (bf16[16,3712]{1,0:T(8,128)(2,1)}, bf16[16,3712]{1,0:T(8,128)(2,1)}, u32[]{:S(2)}, u32[]{:S(2)}) collective-permute-start(bf16[16,3712]{1,0:T(8,128)(2,1)} %get-tuple-element.39), channel_id=1, source_target_pairs={{0,4},{1,5},{2,6},{3,7},{4,0},{5,1},{6,2},{7,3},{8,12},{9,13},{10,... | collective-permute-start | bytes 356360 | tf_op jit(solution)/shard_map/ppermute | solution.py:45
  6.9 18.6 %collective-permute-start.10 = (bf16[16,3712]{1,0:T(8,128)(2,1)}, bf16[16,3712]{1,0:T(8,128)(2,1)S(1)}, u32[]{:S(2)}, u32[]{:S(2)}) collective-permute-start(bf16[16,3712]{1,0:T(8,128)(2,1)} %get-tuple-element.39), channel_id=1, source_target_pairs={{0,6},{1,7},{2,0},{3,1},{4,2},{5,3},{6,4},{7,5},{8,14},{9,15},{10,... | collective-permute-start | bytes 356360 | tf_op jit(solution)/shard_map/ppermute | solution.py:45
  8.4 18.4 %collective-permute-start = (bf16[16,3712]{1,0:T(8,128)(2,1)}, bf16[16,3712]{1,0:T(8,128)(2,1)S(1)}, u32[]{:S(2)}, u32[]{:S(2)}) collective-permute-start(bf16[16,3712]{1,0:T(8,128)(2,1)} %get-tuple-element.37), channel_id=1, source_target_pairs={{0,8},{1,33},{2,10},{3,35},{4,12},{5,37},{6,14},{7,39},{8,16},{9,4... | collective-permute-start | bytes 356360 | tf_op jit(solution)/shard_map/ppermute | solution.py:45
  10.0 17.7 %collective-permute-start.1 = (bf16[16,3712]{1,0:T(8,128)(2,1)}, bf16[16,3712]{1,0:T(8,128)(2,1)S(1)}, u32[]{:S(2)}, u32[]{:S(2)}) collective-permute-start(bf16[16,3712]{1,0:T(8,128)(2,1)} %get-tuple-element.37), channel_id=1, source_target_pairs={{0,16},{1,65},{2,18},{3,67},{4,20},{5,69},{6,22},{7,71},{8,24},{9,... | collective-permute-start | bytes 356360 | tf_op jit(solution)/shard_map/ppermute | solution.py:45
  23.4 27.4 %collective-permute-start.6 = (bf16[576,256]{1,0:T(8,128)(2,1)S(1)}, bf16[576,256]{1,0:T(8,128)(2,1)S(1)}, u32[]{:S(2)}, u32[]{:S(2)}) collective-permute-start(bf16[576,256]{1,0:T(8,128)(2,1)S(1)} %dynamic-slice_bitcast_fusion), channel_id=1, source_target_pairs={{0,2},{1,5},{2,4},{3,7},{4,6},{5,9},{6,8},{7,11},{8,10},{9,13},{10... | collective-permute-start | bytes 884744 | tf_op jit(solution)/shard_map/ppermute | solution.py:406
  26.1 19.3 %collective-permute-start.11 = (bf16[64,3712]{1,0:T(8,128)(2,1)}, bf16[64,3712]{1,0:T(8,128)(2,1)S(1)}, u32[]{:S(2)}, u32[]{:S(2)}) collective-permute-start(bf16[64,3712]{1,0:T(8,128)(2,1)} %constant_dynamic-update-slice_fusion.4.refs_0_), channel_id=1, source_target_pairs={{0,8},{1,33},{2,10},{3,35},{4,12},{5,37},{6,14},{7,39},{8,16},{9,4... | collective-permute-start | bytes 1425416 | tf_op jit(solution)/shard_map/ppermute | solution.py:45
  26.8 18.7 %collective-permute-start.12 = (bf16[64,3712]{1,0:T(8,128)(2,1)}, bf16[64,3712]{1,0:T(8,128)(2,1)S(1)}, u32[]{:S(2)}, u32[]{:S(2)}) collective-permute-start(bf16[64,3712]{1,0:T(8,128)(2,1)} %constant_dynamic-update-slice_fusion.4.refs_0_), channel_id=1, source_target_pairs={{0,16},{1,65},{2,18},{3,67},{4,20},{5,69},{6,22},{7,71},{8,24},{9,... | collective-permute-start | bytes 1425416 | tf_op jit(solution)/shard_map/ppermute | solution.py:45
  27.6 17.8 %collective-permute-start.13 = (bf16[64,3712]{1,0:T(8,128)(2,1)}, bf16[64,3712]{1,0:T(8,128)(2,1)S(1)}, u32[]{:S(2)}, u32[]{:S(2)}) collective-permute-start(bf16[64,3712]{1,0:T(8,128)(2,1)} %constant_dynamic-update-slice_fusion.4.refs_0_), channel_id=1, source_target_pairs={{0,24},{1,97},{2,26},{3,99},{4,28},{5,101},{6,30},{7,103},{8,0},{9... | collective-permute-start | bytes 1425416 | tf_op jit(solution)/shard_map/ppermute | solution.py:45
  29.6 25.3 %collective-permute-start.3 = (bf16[64,3712]{1,0:T(8,128)(2,1)S(1)}, bf16[64,3712]{1,0:T(8,128)(2,1)S(1)}, u32[]{:S(2)}, u32[]{:S(2)}) collective-permute-start(bf16[64,3712]{1,0:T(8,128)(2,1)S(1)} %constant_dynamic-update-slice_fusion.refs_0_), channel_id=1, source_target_pairs={{0,2},{1,3},{2,4},{3,5},{4,6},{5,7},{6,0},{7,1},{8,10},{9,11},{10,... | collective-permute-start | bytes 1425416 | tf_op jit(solution)/shard_map/ppermute | solution.py:45
  48.7 31.6 %collective-permute-start.14 = (bf16[128,3584]{1,0:T(8,128)(2,1)S(1)}, bf16[128,3584]{1,0:T(8,128)(2,1)S(1)}, u32[]{:S(2)}, u32[]{:S(2)}) collective-permute-start(bf16[128,3584]{1,0:T(8,128)(2,1)S(1)} %get-tuple-element.41), channel_id=1, source_target_pairs={{0,32},{1,9},{2,34},{3,11},{4,36},{5,13},{6,38},{7,15},{8,40},{9,1... | collective-permute-start | bytes 2752520 | tf_op jit(solution)/shard_map/ppermute | solution.py:45
  50.7 32.2 %collective-permute-start.15 = (bf16[128,3584]{1,0:T(8,128)(2,1)S(1)}, bf16[128,3584]{1,0:T(8,128)(2,1)S(1)}, u32[]{:S(2)}, u32[]{:S(2)}) collective-permute-start(bf16[128,3584]{1,0:T(8,128)(2,1)S(1)} %get-tuple-element.42), channel_id=1, source_target_pairs={{0,64},{1,17},{2,66},{3,19},{4,68},{5,21},{6,70},{7,23},{8,72},{9,... | collective-permute-start | bytes 2752520 | tf_op jit(solution)/shard_map/ppermute | solution.py:45
  53.4 29.5 %collective-permute-start.16 = (bf16[128,3584]{1,0:T(8,128)(2,1)S(1)}, bf16[128,3584]{1,0:T(8,128)(2,1)S(1)}, u32[]{:S(2)}, u32[]{:S(2)}) collective-permute-start(bf16[128,3584]{1,0:T(8,128)(2,1)S(1)} %get-tuple-element.43), channel_id=1, source_target_pairs={{0,96},{1,25},{2,98},{3,27},{4,100},{5,29},{6,102},{7,31},{8,104},... | collective-permute-start | bytes 2752520 | tf_op jit(solution)/shard_map/ppermute | solution.py:45
  54.8 18.8 %collective-permute-start.4 = (bf16[64,3712]{1,0:T(8,128)(2,1)S(1)}, bf16[64,3712]{1,0:T(8,128)(2,1)S(1)}, u32[]{:S(2)}, u32[]{:S(2)}) collective-permute-start(bf16[64,3712]{1,0:T(8,128)(2,1)S(1)} %constant_dynamic-update-slice_fusion.refs_0_), channel_id=1, source_target_pairs={{0,4},{1,5},{2,6},{3,7},{4,0},{5,1},{6,2},{7,3},{8,12},{9,13},{10,... | collective-permute-start | bytes 1425416 | tf_op jit(solution)/shard_map/ppermute | solution.py:45
  54.9 20.5 %collective-permute-start.5 = (bf16[64,3712]{1,0:T(8,128)(2,1)S(1)}, bf16[64,3712]{1,0:T(8,128)(2,1)S(1)}, u32[]{:S(2)}, u32[]{:S(2)}) collective-permute-start(bf16[64,3712]{1,0:T(8,128)(2,1)S(1)} %constant_dynamic-update-slice_fusion.refs_0_), channel_id=1, source_target_pairs={{0,6},{1,7},{2,0},{3,1},{4,2},{5,3},{6,4},{7,5},{8,14},{9,15},{10,... | collective-permute-start | bytes 1425416 | tf_op jit(solution)/shard_map/ppermute | solution.py:45
  77.3 24.5 %collective-permute-start.28 = (bf16[128,3584]{1,0:T(8,128)(2,1)S(1)}, bf16[128,3584]{1,0:T(8,128)(2,1)S(1)}, u32[]{:S(2)}, u32[]{:S(2)}) collective-permute-start(bf16[128,3584]{1,0:T(8,128)(2,1)S(1)} %get-tuple-element.59), channel_id=1, source_target_pairs={{0,32},{1,9},{2,34},{3,11},{4,36},{5,13},{6,38},{7,15},{8,40},{9,1... | collective-permute-start | bytes 2752520 | tf_op jit(solution)/shard_map/ppermute | solution.py:45
  79.0 22.8 %collective-permute-start.29 = (bf16[128,3584]{1,0:T(8,128)(2,1)S(1)}, bf16[128,3584]{1,0:T(8,128)(2,1)S(1)}, u32[]{:S(2)}, u32[]{:S(2)}) collective-permute-start(bf16[128,3584]{1,0:T(8,128)(2,1)S(1)} %get-tuple-element.60), channel_id=1, source_target_pairs={{0,64},{1,17},{2,66},{3,19},{4,68},{5,21},{6,70},{7,23},{8,72},{9,... | collective-permute-start | bytes 2752520 | tf_op jit(solution)/shard_map/ppermute | solution.py:45
  80.4 22.3 %collective-permute-start.30 = (bf16[128,3584]{1,0:T(8,128)(2,1)S(1)}, bf16[128,3584]{1,0:T(8,128)(2,1)S(1)}, u32[]{:S(2)}, u32[]{:S(2)}) collective-permute-start(bf16[128,3584]{1,0:T(8,128)(2,1)S(1)} %get-tuple-element.61), channel_id=1, source_target_pairs={{0,96},{1,25},{2,98},{3,27},{4,100},{5,29},{6,102},{7,31},{8,104},... | collective-permute-start | bytes 2752520 | tf_op jit(solution)/shard_map/ppermute | solution.py:45
  87.6 20.3 %collective-permute-start.17 = (f32[512,512]{1,0:T(8,128)S(1)}, f32[512,512]{1,0:T(8,128)S(1)}, u32[]{:S(2)}, u32[]{:S(2)}) collective-permute-start(f32[512,512]{1,0:T(8,128)S(1)} %get-tuple-element.44.refs_0_), channel_id=1, source_target_pairs={{0,1},{1,0},{2,3},{3,2},{4,5},{5,4},{6,7},{7,6},{8,9},{9,8},{10,11... | collective-permute-start | bytes 3145736 | tf_op jit(solution)/shard_map/ppermute | solution.py:371
  87.7 20.2 %collective-permute-start.18 = (f32[512,512]{1,0:T(8,128)S(1)}, f32[512,512]{1,0:T(8,128)S(1)}, u32[]{:S(2)}, u32[]{:S(2)}) collective-permute-start(f32[512,512]{1,0:T(8,128)S(1)} %get-tuple-element.45.refs_2_), channel_id=1, source_target_pairs={{0,1},{1,0},{2,3},{3,2},{4,5},{5,4},{6,7},{7,6},{8,9},{9,8},{10,11... | collective-permute-start | bytes 3145736 | tf_op jit(solution)/shard_map/ppermute | solution.py:371
  110.6 23.5 %collective-permute-start.19 = (bf16[128,3584]{1,0:T(8,128)(2,1)S(1)}, bf16[128,3584]{1,0:T(8,128)(2,1)S(1)}, u32[]{:S(2)}, u32[]{:S(2)}) collective-permute-start(bf16[128,3584]{1,0:T(8,128)(2,1)S(1)} %get-tuple-element.47), channel_id=1, source_target_pairs={{0,96},{1,25},{2,98},{3,27},{4,100},{5,29},{6,102},{7,31},{8,104},... | collective-permute-start | bytes 2752520 | tf_op jit(solution)/shard_map/ppermute | solution.py:45
  113.3 20.8 %collective-permute-start.20 = (bf16[128,3584]{1,0:T(8,128)(2,1)S(1)}, bf16[128,3584]{1,0:T(8,128)(2,1)S(1)}, u32[]{:S(2)}, u32[]{:S(2)}) collective-permute-start(bf16[128,3584]{1,0:T(8,128)(2,1)S(1)} %get-tuple-element.48), channel_id=1, source_target_pairs={{0,64},{1,17},{2,66},{3,19},{4,68},{5,21},{6,70},{7,23},{8,72},{9,... | collective-permute-start | bytes 2752520 | tf_op jit(solution)/shard_map/ppermute | solution.py:45
  114.8 23.3 %collective-permute-start.21 = (bf16[128,3584]{1,0:T(8,128)(2,1)S(1)}, bf16[128,3584]{1,0:T(8,128)(2,1)S(1)}, u32[]{:S(2)}, u32[]{:S(2)}) collective-permute-start(bf16[128,3584]{1,0:T(8,128)(2,1)S(1)} %get-tuple-element.49), channel_id=1, source_target_pairs={{0,32},{1,9},{2,34},{3,11},{4,36},{5,13},{6,38},{7,15},{8,40},{9,1... | collective-permute-start | bytes 2752520 | tf_op jit(solution)/shard_map/ppermute | solution.py:45
  117.9 35.9 %collective-permute-start.33 = (bf16[128,3584]{1,0:T(8,128)(2,1)S(1)}, bf16[128,3584]{1,0:T(8,128)(2,1)S(1)}, u32[]{:S(2)}, u32[]{:S(2)}) collective-permute-start(bf16[128,3584]{1,0:T(8,128)(2,1)S(1)} %get-tuple-element.65), channel_id=1, source_target_pairs={{0,96},{1,25},{2,98},{3,27},{4,100},{5,29},{6,102},{7,31},{8,104},... | collective-permute-start | bytes 2752520 | tf_op jit(solution)/shard_map/ppermute | solution.py:45
  120.9 33.1 %collective-permute-start.34 = (bf16[128,3584]{1,0:T(8,128)(2,1)S(1)}, bf16[128,3584]{1,0:T(8,128)(2,1)S(1)}, u32[]{:S(2)}, u32[]{:S(2)}) collective-permute-start(bf16[128,3584]{1,0:T(8,128)(2,1)S(1)} %get-tuple-element.66), channel_id=1, source_target_pairs={{0,64},{1,17},{2,66},{3,19},{4,68},{5,21},{6,70},{7,23},{8,72},{9,... | collective-permute-start | bytes 2752520 | tf_op jit(solution)/shard_map/ppermute | solution.py:45
  134.1 23.7 %collective-permute-start.35 = (bf16[128,3584]{1,0:T(8,128)(2,1)S(1)}, bf16[128,3584]{1,0:T(8,128)(2,1)S(1)}, u32[]{:S(2)}, u32[]{:S(2)}) collective-permute-start(bf16[128,3584]{1,0:T(8,128)(2,1)S(1)} %get-tuple-element.67), channel_id=1, source_target_pairs={{0,32},{1,9},{2,34},{3,11},{4,36},{5,13},{6,38},{7,15},{8,40},{9,1... | collective-permute-start | bytes 2752520 | tf_op jit(solution)/shard_map/ppermute | solution.py:45
  141.0 22.7 %collective-permute-start.22 = (bf16[64,3584]{1,0:T(8,128)(2,1)S(1)}, bf16[64,3584]{1,0:T(8,128)(2,1)S(1)}, u32[]{:S(2)}, u32[]{:S(2)}) collective-permute-start(bf16[64,3584]{1,0:T(8,128)(2,1)S(1)} %get-tuple-element.51), channel_id=1, source_target_pairs={{0,6},{1,7},{2,0},{3,1},{4,2},{5,3},{6,4},{7,5},{8,14},{9,15},{10,... | collective-permute-start | bytes 1376264 | tf_op jit(solution)/shard_map/ppermute | solution.py:45
  143.6 21.1 %collective-permute-start.23 = (bf16[64,3584]{1,0:T(8,128)(2,1)S(1)}, bf16[64,3584]{1,0:T(8,128)(2,1)S(1)}, u32[]{:S(2)}, u32[]{:S(2)}) collective-permute-start(bf16[64,3584]{1,0:T(8,128)(2,1)S(1)} %get-tuple-element.52), channel_id=1, source_target_pairs={{0,4},{1,5},{2,6},{3,7},{4,0},{5,1},{6,2},{7,3},{8,12},{9,13},{10,... | collective-permute-start | bytes 1376264 | tf_op jit(solution)/shard_map/ppermute | solution.py:45
  153.8 12.2 %collective-permute-start.24 = (bf16[64,3584]{1,0:T(8,128)(2,1)S(1)}, bf16[64,3584]{1,0:T(8,128)(2,1)S(1)}, u32[]{:S(2)}, u32[]{:S(2)}) collective-permute-start(bf16[64,3584]{1,0:T(8,128)(2,1)S(1)} %get-tuple-element.53), channel_id=1, source_target_pairs={{0,2},{1,3},{2,4},{3,5},{4,6},{5,7},{6,0},{7,1},{8,10},{9,11},{10,... | collective-permute-start | bytes 1376264 | tf_op jit(solution)/shard_map/ppermute | solution.py:45
  160.7 12.9 %collective-permute-start.36 = (bf16[64,3584]{1,0:T(8,128)(2,1)S(1)}, bf16[64,3584]{1,0:T(8,128)(2,1)S(1)}, u32[]{:S(2)}, u32[]{:S(2)}) collective-permute-start(bf16[64,3584]{1,0:T(8,128)(2,1)S(1)} %get-tuple-element.69), channel_id=1, source_target_pairs={{0,24},{1,97},{2,26},{3,99},{4,28},{5,101},{6,30},{7,103},{8,0},{9... | collective-permute-start | bytes 1376264 | tf_op jit(solution)/shard_map/ppermute | solution.py:45
  163.6 13.9 %collective-permute-start.38 = (bf16[64,3584]{1,0:T(8,128)(2,1)S(1)}, bf16[64,3584]{1,0:T(8,128)(2,1)S(1)}, u32[]{:S(2)}, u32[]{:S(2)}) collective-permute-start(bf16[64,3584]{1,0:T(8,128)(2,1)S(1)} %get-tuple-element.71), channel_id=1, source_target_pairs={{0,8},{1,33},{2,10},{3,35},{4,12},{5,37},{6,14},{7,39},{8,16},{9,4... | collective-permute-start | bytes 1376264 | tf_op jit(solution)/shard_map/ppermute | solution.py:45
  166.2 14.3 %collective-permute-start.25 = (bf16[16,3584]{1,0:T(8,128)(2,1)S(1)}, bf16[16,3584]{1,0:T(8,128)(2,1)S(1)}, u32[]{:S(2)}, u32[]{:S(2)}) collective-permute-start(bf16[16,3584]{1,0:T(8,128)(2,1)S(1)} %get-tuple-element.72), channel_id=1, source_target_pairs={{0,24},{1,97},{2,26},{3,99},{4,28},{5,101},{6,30},{7,103},{8,0},{9... | collective-permute-start | bytes 344072 | tf_op jit(solution)/shard_map/ppermute | solution.py:45
  (33 other events, 594.7 us)
where the time goes:
time: 189 us; the launch traced here: 188 us
  waiting for transfers between devices  77.1 us (41%)
  starting transfers between devices  52.5 us (28%)
  Pallas kernels  38.5 us (20%)
  local copies, waits for them, and re-layouts  13.9 us (7%)
  between operations  3.59 us (2%)
  other arithmetic  2.81 us (1%)
    ppermute x36, waiting for transfers between devices, hop(): return lax.ppermute(value, BOTH, pairs)  77.1 us
    ppermute x36, starting transfers between devices, hop(): return lax.ppermute(value, BOTH, pairs)  50.7 us
    pallas_call x1, Pallas kernels, attend(): pl.pallas_call(attend_kernel, grid_spec=pltpu.PrefetchScalarGridSpec(num_...  12.4 us
    unnamed x53, local copies, waits for them, and re-layouts  10.9 us
    pallas_call x2, Pallas kernels, widen(): pl.pallas_call(widen_kernel, in_specs=[IN_SMEM] + [IN_VMEM] * (SIDE + 2),...  9.22 us
    pallas_call x2, Pallas kernels, mix(): pl.pallas_call(functools.partial(mix_kernel, by_inner), in_specs=[IN_SMEM...  5.75 us
    pallas_call x2, Pallas kernels, narrow(): pl.pallas_call(narrow_kernel, in_specs=[IN_SMEM] + [IN_VMEM] * 5, out_spe...  5.45 us
  transfers between devices with their start and end apart: 42, of which 14 were waited for; matrix products, arithmetic and copies ran while one was open for 6% of the time, Pallas kernels for 19%

commit v1 on v0

v1 whole, which is shorter than its diff:
```python
import functools

import jax
import jax.numpy as jnp
from jax import lax
from jax.experimental import pallas as pl
from jax.experimental.pallas import tpu as pltpu
from jax.sharding import PartitionSpec as P

LAT = 512
STEPS = 4
MOST = 4
SIDE = 4
RANKS = SIDE * SIDE
MOVED = 256
TILE = 512
BATCHES = ((0, 1), (2, 3))
ORDERS = (("x", "y", "z"), ("x", "z", "y"))
STRIDE = {"z": 16, "y": 4, "x": 1}
BOTH = ("wide", "narrow")
MIB = 1024 * 1024
SHARE = 0.1


def cost(micros):
    return pl.CostEstimate(flops=int(micros * SHARE * 1.1e9), bytes_accessed=1, transcendentals=0)


IN_VMEM = pl.BlockSpec(memory_space=pltpu.VMEM)

score_scale = 192.0 ** (-0.5)
route_scale = 2.5


def params(mib):
    return pltpu.CompilerParams(vmem_limit_bytes=mib * MIB)


def moved_along(rank, axis, steps):
    place = rank // STRIDE[axis] % SIDE
    return rank + ((place + steps) % SIDE - place) * STRIDE[axis]


def hop(value, axes, steps):
    if steps == 0:
        return value
    pairs = [
        (rank * 2 + core, moved_along(rank, axes[core], steps) * 2 + core)
        for rank in range(64)
        for core in range(2)
    ]
    return lax.ppermute(value, BOTH, pairs)


def axes_at(stage):
    return tuple(order[stage] for order in ORDERS)


def by_core(core, first, second):
    return jnp.where(core == 0, first, second)


def reached_experts():
    rank, core = lax.axis_index("wide"), lax.axis_index("narrow")
    first, second = axes_at(2)
    return [
        by_core(core, moved_along(rank, first, steps) // 2, moved_along(rank, second, steps) // 2)
        for steps in range(SIDE)
    ]


def block_strides():
    core = lax.axis_index("narrow")
    return [by_core(core, *(STRIDE[axis] for axis in axes_at(level))) for level in (2, 1, 0)]


def attend_kernel(
    lengths, receivers, query_hbm, cache_hbm, moved_ref, other_ref, fresh_ref, out_ref, query_held, cache_held, sems
):
    slot = pl.program_id(0)
    count = pl.num_programs(0)

    def copies(index):
        held = lax.rem(index, 2)
        return (
            pltpu.make_async_copy(query_hbm.at[:, index], query_held.at[held], sems.at[held, 0]),
            pltpu.make_async_copy(cache_hbm.at[index], cache_held.at[held], sems.at[held, 1]),
        )

    @pl.when(slot == 0)
    def _():
        for copy in copies(slot):
            copy.start()

    @pl.when(slot + 1 < count)
    def _():
        for copy in copies(slot + 1):
            copy.start()

    for copy in copies(slot):
        copy.wait()
    now = lax.rem(slot, 2)
    query_ref, cache_ref = query_held.at[now], cache_held.at[now]
    length = lengths[slot]
    blocks = (length + 255) // 256
    steps, heads, width = query_ref.shape
    rows = steps * heads
    slots = fresh_ref.shape[1]
    core = lax.axis_index("narrow")
    per_slot = cache_ref.shape[1] // 32
    contract_last = (((1,), (1,)), ((), ()))

    def run(count):
        query = query_ref[...].reshape(rows, width)
        fresh = fresh_ref[...].reshape(-1, width)
        fresh_scores = (
            lax.dot_general(query, fresh, contract_last, preferred_element_type=jnp.float32)
            * score_scale
        )
        row_step = lax.broadcasted_iota(jnp.int32, fresh_scores.shape, 0) // heads
        column = lax.broadcasted_iota(jnp.int32, fresh_scores.shape, 1)
        allowed = (column // slots <= row_step) & (column % slots == slot)
        fresh_scores = jnp.where(allowed, fresh_scores, -jnp.inf)
        peak = jnp.max(fresh_scores, axis=1, keepdims=True)
        keys = []
        scores = []
        for index in range(count):
            key = cache_ref[:, index * 256 : (index + 1) * 256]
            if count == 1:
                key = jnp.where(slot == receivers[core, 0] // per_slot, moved_ref[...], key)
                key = jnp.where(slot == receivers[1 - core, 0] // per_slot, other_ref[...], key)
            score = jnp.dot(query, key, preferred_element_type=jnp.float32) * score_scale
            if index == count - 1:
                position = lax.broadcasted_iota(jnp.int32, score.shape, 1) + index * 256
                score = jnp.where(position < length, score, -jnp.inf)
            peak = jnp.maximum(peak, jnp.max(score, axis=1, keepdims=True))
            keys.append(key)
            scores.append(score)
        fresh_exp = jnp.exp(fresh_scores - peak)
        total = jnp.sum(fresh_exp, axis=1, keepdims=True)
        exps = []
        for score in scores:
            weight = jnp.exp(score - peak)
            total = total + jnp.sum(weight, axis=1, keepdims=True)
            exps.append(weight)
        inverse = 1.0 / total
        context = jnp.dot(
            (fresh_exp * inverse).astype(jnp.bfloat16),
            fresh[:, :LAT],
            preferred_element_type=jnp.float32,
        )
        for weight, key in zip(exps, keys):
            context = context + lax.dot_general(
                (weight * inverse).astype(jnp.bfloat16),
                key[:LAT],
                contract_last,
                preferred_element_type=jnp.float32,
            )
        out_ref[...] = context.astype(jnp.bfloat16).reshape(out_ref.shape)

    for count in range(5):
        pl.when(blocks == count)(functools.partial(run, count))


def attend(queries, cache, lengths, receivers, moved, other, new_latent):
    steps, slots, heads, width = queries.shape
    in_place = pl.BlockSpec(memory_space=pltpu.HBM)
    return pl.pallas_call(
        attend_kernel,
        grid_spec=pltpu.PrefetchScalarGridSpec(
            num_scalar_prefetch=2,
            grid=(slots,),
            in_specs=[in_place, in_place, IN_VMEM, IN_VMEM, IN_VMEM],
            out_specs=pl.BlockSpec((steps, 1, heads, LAT), lambda i, *_: (0, i, 0, 0)),
            scratch_shapes=[
                pltpu.VMEM((2, steps, heads, width), jnp.bfloat16),
                pltpu.VMEM((2,) + cache.shape[1:], jnp.bfloat16),
                pltpu.SemaphoreType.DMA((2, 2)),
            ],
        ),
        out_shape=jax.ShapeDtypeStruct((steps, slots, heads, LAT), jnp.bfloat16),
        compiler_params=params(52),
        cost_estimate=cost(12),
        name="attend",
    )(lengths, receivers, queries, cache, moved, other, new_latent)


def pack_kernel(
    send_ref, token_hbm, id_hbm, affinity_hbm, cache_hbm, out_ref, moving_ref, token_ref, id_ref, affinity_ref, sems
):
    steps, requests, half_width = token_ref.shape
    topk = id_ref.shape[2]
    rows = steps * requests
    sending = send_ref[lax.axis_index("narrow"), 0] // (cache_hbm.shape[2] // 32)
    pairs = [
        (id_hbm, id_ref),
        (affinity_hbm, affinity_ref),
        (token_hbm, token_ref),
        (cache_hbm.at[sending, :, pl.ds(0, MOVED)], moving_ref),
    ]
    copies = [pltpu.make_async_copy(*pair, sems.at[index]) for index, pair in enumerate(pairs)]
    for copy in copies:
        copy.start()
    copies[0].wait()
    copies[1].wait()
    ids = id_ref[...].reshape(rows, topk)
    affinity = affinity_ref[...].reshape(rows, topk)
    share = route_scale * affinity / jnp.sum(affinity, axis=1, keepdims=True)
    high = share.astype(jnp.bfloat16).astype(jnp.float32)
    low = share - high
    lane = lax.broadcasted_iota(jnp.int32, (rows, 128), 1)
    hot = jnp.zeros((rows, 128), jnp.float32)
    shares = jnp.zeros((rows, 128), jnp.float32)
    for k in range(topk):
        named = ids[:, k : k + 1]
        hot = jnp.where(lane == named, 1.0, hot)
        shares = jnp.where(lane == named + 32, high[:, k : k + 1], shares)
        shares = jnp.where(lane == named + 64, low[:, k : k + 1], shares)
    row = lax.broadcasted_iota(jnp.int32, (rows, rows), 0)
    other = lax.broadcasted_iota(jnp.int32, (rows, rows), 1)
    earlier = ((other < row) & (row // requests == other // requests)).astype(jnp.bfloat16)
    before = jnp.dot(earlier, hot.astype(jnp.bfloat16), preferred_element_type=jnp.float32)
    routing = jnp.where(lane < 32, jnp.where(hot > 0.5, before, -1.0), shares).astype(jnp.bfloat16)
    copies[2].wait()
    out_ref[:, :half_width] = token_ref[...].reshape(rows, half_width)
    out_ref[:, half_width:] = routing
    copies[3].wait()


def pack(mig_send, tokens, expert_ids, affinity, keys_last):
    steps, requests, half_width = tokens.shape
    in_place = pl.BlockSpec(memory_space=pltpu.HBM)
    return pl.pallas_call(
        pack_kernel,
        in_specs=[pl.BlockSpec(memory_space=pltpu.SMEM)] + [in_place] * 4,
        out_specs=[IN_VMEM] * 2,
        out_shape=[
            jax.ShapeDtypeStruct((steps * requests, half_width + 128), jnp.bfloat16),
            jax.ShapeDtypeStruct((keys_last.shape[1], MOVED), jnp.bfloat16),
        ],
        scratch_shapes=[
            pltpu.VMEM(tokens.shape, jnp.bfloat16),
            pltpu.VMEM(expert_ids.shape, jnp.int32),
            pltpu.VMEM(affinity.shape, jnp.float32),
            pltpu.SemaphoreType.DMA((4,)),
        ],
        compiler_params=params(60),
        cost_estimate=cost(3),
        name="pack",
    )(mig_send, tokens, expert_ids, affinity, keys_last)


def stack_kernel(*refs):
    piece_refs, out_ref = refs[:SIDE], refs[SIDE]
    each = piece_refs[0].shape[0]
    for index, ref in enumerate(piece_refs):
        out_ref[index * each : (index + 1) * each, :] = ref[...]


def stack(pieces):
    rows, width = pieces[0].shape
    return pl.pallas_call(
        stack_kernel,
        in_specs=[IN_VMEM] * SIDE,
        out_specs=IN_VMEM,
        out_shape=jax.ShapeDtypeStruct((SIDE * rows, width), jnp.bfloat16),
        compiler_params=params(4),
        cost_estimate=cost(0.6),
        name="stack",
    )(*pieces)


def half_rows(refs, half, columns):
    each = refs[0].shape[0] // SIDE
    start = half * each // 2
    return jnp.concatenate(
        [
            ref[rank * each + start : rank * each + start + each // 2, columns]
            for ref in refs
            for rank in range(SIDE)
        ],
        axis=0,
    )


def four(rows, width):
    return [jax.ShapeDtypeStruct((rows, width), jnp.bfloat16)] * SIDE


def along_lanes(aux, wanted, shape, transposed):
    if transposed:
        lane = lax.broadcasted_iota(jnp.int32, (shape[0], 128), 1)
        chosen = (lane == wanted).astype(jnp.bfloat16)
        return lax.dot_general(
            chosen, aux, (((1,), (1,)), ((), ())), preferred_element_type=jnp.float32
        )
    lane = lax.broadcasted_iota(jnp.int32, (128, shape[1]), 0)
    chosen = (lane == wanted).astype(jnp.bfloat16)
    return jnp.dot(aux, chosen, preferred_element_type=jnp.float32)


def placed(aux, expert, shape, transposed):
    place = along_lanes(aux, expert, shape, transposed).astype(jnp.int32)
    row = lax.broadcasted_iota(jnp.int32, shape, 1 if transposed else 0)
    cell = lax.broadcasted_iota(jnp.int32, shape, 0 if transposed else 1)
    return (place >= 0) & (row // 8 * MOST + place == cell)


def pick_kernel(half, *refs):
    experts = reached_experts()
    piece_refs, out_refs = refs[:SIDE], refs[SIDE:]
    half_width = out_refs[0].shape[1]
    aux = half_rows(piece_refs, half, pl.ds(half_width, 128))
    rows = aux.shape[0]
    pickers = [
        placed(aux, experts[index], (rows // 2, rows), True).astype(jnp.bfloat16) for index in range(SIDE)
    ]
    for start in range(0, half_width, TILE):
        values = half_rows(piece_refs, half, pl.ds(start, TILE))
        for index in range(SIDE):
            out_refs[index][:, start : start + TILE] = jnp.dot(
                pickers[index], values, preferred_element_type=jnp.float32
            ).astype(jnp.bfloat16)


def pick(pieces, half, half_width):
    rows = pieces[0].shape[0] * SIDE // 2
    return pl.pallas_call(
        functools.partial(pick_kernel, half),
        in_specs=[IN_VMEM] * SIDE,
        out_specs=[IN_VMEM] * SIDE,
        out_shape=four(rows // 2, half_width),
        compiler_params=params(12),
        cost_estimate=cost(2),
        name="pick",
    )(*pieces)


def mix_kernel(half, by_inner, *refs):
    experts = reached_experts()
    piece_refs, cell_refs, out_refs = refs[:SIDE], refs[SIDE:-SIDE], refs[-SIDE:]
    rows_each, half_width = out_refs[0].shape
    rows = rows_each * SIDE
    cells = rows // 2
    each = rows_each // SIDE
    aux = half_rows(piece_refs, half, pl.ds(half_width, 128))
    mixers = []
    for index in range(SIDE):
        chosen = placed(aux, experts[index], (rows, cells), False)
        for level in (1, 2):
            share = along_lanes(aux, experts[index] + 32 * level, (rows, cells), False)
            mixers.append(jnp.where(chosen, share, 0.0).astype(jnp.bfloat16))
    high = jnp.concatenate(mixers[0::2], axis=1)
    low = jnp.concatenate(mixers[1::2], axis=1)
    for start in range(0, half_width, TILE):
        answers = jnp.concatenate(
            [ref[:, start : start + TILE] for ref in cell_refs], axis=0
        )
        mixed = jnp.dot(high, answers, preferred_element_type=jnp.float32)
        mixed = mixed + jnp.dot(low, answers, preferred_element_type=jnp.float32)
        mixed = mixed.astype(jnp.bfloat16)
        for outer in range(SIDE):
            for inner in range(SIDE):
                block = mixed[(outer * SIDE + inner) * each : (outer * SIDE + inner + 1) * each]
                piece, place = (inner, outer) if by_inner else (outer, inner)
                out_refs[piece][place * each : (place + 1) * each, start : start + TILE] = block


def mix(pieces, answers, half, by_inner):
    rows = pieces[0].shape[0] * SIDE // 2
    half_width = answers[0].shape[1]
    return pl.pallas_call(
        functools.partial(mix_kernel, half, by_inner),
        in_specs=[IN_VMEM] * 2 * SIDE,
        out_specs=[IN_VMEM] * SIDE,
        out_shape=four(rows // SIDE, half_width),
        compiler_params=params(16),
        cost_estimate=cost(2.5),
        name="mix",
    )(*pieces, *answers)


def widen_kernel(*refs):
    row_refs, (gate_ref, up_ref, *out_refs) = refs[:SIDE], refs[SIDE:]
    strides = block_strides()
    units = gate_ref.shape[1]
    rows = jnp.concatenate([ref[...] for ref in row_refs], axis=0)
    each = rows.shape[0] // SIDE**3
    for weight_ref, out_ref, sent_ref in zip((gate_ref, up_ref), out_refs[:2], out_refs[2:]):
        for start in range(0, units, 256):
            columns = pl.ds(start, 256)
            result = jnp.dot(
                rows, weight_ref[:, start : start + 256], preferred_element_type=jnp.float32
            )
            for outer in range(SIDE):
                for middle in range(SIDE):
                    for inner in range(SIDE):
                        block = (outer * SIDE + middle) * SIDE + inner
                        place = outer * strides[0] + middle * strides[1] + inner * strides[2]
                        place = pl.multiple_of(place * each, each)
                        out_ref[pl.ds(place, each), columns] = result[
                            block * each : (block + 1) * each
                        ]
            sent_ref[:, columns] = out_ref[:, columns].astype(jnp.bfloat16)


def widen(rows, gate_weight, up_weight):
    total = sum(array.shape[0] for array in rows)
    units = gate_weight.shape[1]
    return pl.pallas_call(
        widen_kernel,
        in_specs=[IN_VMEM] * (len(rows) + 2),
        out_specs=[IN_VMEM] * 4,
        out_shape=[
            jax.ShapeDtypeStruct((total, units), kind)
            for kind in (jnp.float32, jnp.float32, jnp.bfloat16, jnp.bfloat16)
        ],
        compiler_params=params(26),
        cost_estimate=cost(5),
        name="widen",
    )(*rows, gate_weight, up_weight)


def narrow_kernel(gate_own, up_own, gate_other, up_other, weight_ref, *refs):
    out_refs, hidden, wide = refs[:-2], *refs[-2:]
    strides = block_strides()
    units, half_width = weight_ref.shape
    total = wide.shape[0]
    cells, each = total // SIDE, total // SIDE**3
    wide[:, :units] = gate_own[...] + gate_other[...].astype(jnp.float32)
    wide[:, units:] = up_own[...] + up_other[...].astype(jnp.float32)
    for outer in range(SIDE):
        for middle in range(SIDE):
            parts = []
            for inner in range(SIDE):
                place = outer * strides[0] + middle * strides[1] + inner * strides[2]
                place = pl.ds(pl.multiple_of(place * each, each), each)
                gate = wide[place, :units]
                parts.append(gate / (1.0 + jnp.exp(-gate)) * wide[place, units:])
            block = (outer * SIDE + middle) * SIDE
            hidden[block * each : (block + SIDE) * each, :] = jnp.concatenate(
                parts, axis=0
            ).astype(jnp.bfloat16)
    for start in range(0, half_width, TILE):
        result = jnp.dot(
            hidden[...], weight_ref[:, start : start + TILE], preferred_element_type=jnp.float32
        )
        for index in range(SIDE):
            out_refs[index][:, start : start + TILE] = result[
                index * cells : (index + 1) * cells
            ].astype(jnp.bfloat16)


def narrow(gate_own, up_own, gate_other, up_other, down_weight):
    total = gate_own.shape[0]
    units, half_width = down_weight.shape
    return pl.pallas_call(
        narrow_kernel,
        in_specs=[IN_VMEM] * 5,
        out_specs=[IN_VMEM] * SIDE,
        out_shape=four(total // SIDE, half_width),
        scratch_shapes=[
            pltpu.VMEM((total, units), jnp.bfloat16),
            pltpu.VMEM((total, 2 * units), jnp.float32),
        ],
        compiler_params=params(20),
        cost_estimate=cost(3),
        name="narrow",
    )(gate_own, up_own, gate_other, up_other, down_weight)


def swap_cores(value):
    return lax.ppermute(value, "narrow", [(0, 1), (1, 0)])


def sum_kernel(*refs):
    piece_refs, out_refs = refs[:SIDE], refs[SIDE:]
    total = piece_refs[0][...].astype(jnp.float32)
    for ref in piece_refs[1:]:
        total = total + ref[...].astype(jnp.float32)
    total = total.astype(jnp.bfloat16)
    each = out_refs[0].shape[0]
    for index, out_ref in enumerate(out_refs):
        out_ref[...] = total[index * each : (index + 1) * each]


def add_up(pieces):
    rows, width = pieces[0].shape
    return pl.pallas_call(
        sum_kernel,
        in_specs=[IN_VMEM] * SIDE,
        out_specs=[IN_VMEM] * SIDE,
        out_shape=[jax.ShapeDtypeStruct((rows // SIDE, width), jnp.bfloat16)] * SIDE,
        compiler_params=params(8),
        name="add_up",
    )(*pieces)


def last_kernel(*refs):
    piece_refs, out_ref = refs[:-1], refs[-1]
    count = len(BATCHES)
    requests, width = out_ref.shape[1:]
    for batch in range(count):
        pieces = piece_refs[batch * SIDE : (batch + 1) * SIDE]
        total = pieces[0][...].astype(jnp.float32)
        for ref in pieces[1:]:
            total = total + ref[...].astype(jnp.float32)
        steps = total.shape[0] // requests
        out_ref[batch * steps : (batch + 1) * steps] = total.astype(jnp.bfloat16).reshape(
            steps, requests, width
        )


def add_last(pieces, shape):
    return pl.pallas_call(
        last_kernel,
        in_specs=[IN_VMEM] * len(pieces),
        out_specs=IN_VMEM,
        out_shape=jax.ShapeDtypeStruct(shape, jnp.bfloat16),
        compiler_params=params(6),
        name="add_last",
    )(*pieces)


def in_turn(earlier, later):
    return lax.optimization_barrier((earlier, later))


def body(
    cache,
    lengths,
    mig_send,
    mig_recv,
    mig_count,
    queries,
    new_latent,
    tokens,
    expert_ids,
    affinity,
    gate_weight,
    up_weight,
    down_weight,
):
    half_width = tokens.shape[2]

    def spread(stage, pieces):
        return [hop(piece, axes_at(stage), steps) for steps, piece in enumerate(pieces)]

    def bring(stage, pieces):
        return [hop(piece, axes_at(stage), -steps) for steps, piece in enumerate(pieces)]

    def answer(rows):
        gate, up, sent_gate, sent_up = widen(rows, gate_weight, up_weight)
        return narrow(gate, up, swap_cores(sent_gate), swap_cores(sent_up), down_weight)

    keys_last = jnp.swapaxes(cache, 1, 2)
    own_rows, moving = pack(mig_send[0], tokens, expert_ids, affinity, keys_last)
    pairs = [(r * 2 + j, (r + j + 1) % 64 * 2 + j) for r in range(64) for j in range(2)]
    moved = lax.ppermute(moving, BOTH, pairs)

    row = stack(spread(0, [own_rows] * SIDE))
    (moved, lengths), row = in_turn((moved, lengths), row)
    plane = spread(1, [row] * SIDE)
    context = attend(queries, keys_last, lengths, mig_recv[0], moved, swap_cores(moved), new_latent)
    context, plane = in_turn(context, plane)

    first_cells, second_cells = [spread(2, pick(plane, half, half_width)) for half in range(2)]

    first_answers = answer(first_cells)
    first_answers, second_cells = in_turn(first_answers, second_cells)
    first_answers = bring(2, first_answers)
    second_answers = bring(2, answer(second_cells))
    first = bring(1, add_up(bring(0, mix(plane, first_answers, 0, True))))
    second = bring(0, add_up(bring(1, mix(plane, second_answers, 1, False))))
    return (context, add_last(first + second, tokens.shape))


def solution(mesh):
    specs = (
        P("wide", None, None),
        P("wide"),
        P("wide", None, None),
        P("wide", None, None),
        P("wide", None),
        P(None, "wide", "narrow", None),
        P(None, "wide", None),
        P(None, "wide", "narrow"),
        P(None, "wide", None),
        P(None, "wide", None),
        P("narrow", "wide"),
        P("narrow", "wide"),
        P("wide", "narrow"),
    )
    return jax.shard_map(
        body,
        mesh=mesh,
        in_specs=specs,
        out_specs=(P(None, "wide", "narrow", None), P(None, "wide", "narrow")),
        check_vma=False,
    )
```

time: 189 us -> 181 us (0.958)
  waiting for transfers between devices: 77.1 us -> 94.9 us
  local copies, waits for them, and re-layouts: 13.9 us -> 0.97 us
  starting transfers between devices: 52.5 us -> 43.9 us
  other arithmetic: 2.81 us -> 0 us
  between operations: 3.59 us -> 0.86 us
    ppermute x36 -> x30, waiting for transfers between devices: 77.1 us -> 90.9 us  [hop(): return lax.ppermute(value, BOTH, pairs)]
    unnamed x53 -> x14, local copies, waits for them, and re-layouts: 10.9 us -> 0.97 us
    ppermute x36 -> x30, starting transfers between devices: 50.7 us -> 41.1 us  [hop(): return lax.ppermute(value, BOTH, pairs)]
    ppermute x5, waiting for transfers between devices: 0.01 us -> 4.03 us  [swap_cores(): return lax.ppermute(value, 'narrow', [(0, 1), (1, 0)])]
    pallas_call x1, Pallas kernels: 12.4 us -> 14.4 us  [attend(): pl.pallas_call(attend_kernel, grid_spec=pltpu.PrefetchScalarGridSpec(num_...]
    pallas_call x9 -> x13, Pallas kernels: 26.2 us -> 25.1 us  [the longest x2 8.28 us: widen(): pl.pallas_call(widen_kernel, in_specs=[IN_VMEM] * (len(rows) + 2), out_sp...]
  transfers between devices with their start and end apart: 42 -> 36, of which waited for: 14 -> 19; matrix products, arithmetic and copies ran while one was open for 6% -> 0% of each run, Pallas kernels for 19% -> 19%
where the time goes in v1:
time: 181 us; the launch traced here: 180 us
  waiting for transfers between devices  94.9 us (52%)
  starting transfers between devices  43.9 us (24%)
  Pallas kernels  39.5 us (22%)
    ppermute x30, waiting for transfers between devices, hop(): return lax.ppermute(value, BOTH, pairs)  90.9 us
    ppermute x30, starting transfers between devices, hop(): return lax.ppermute(value, BOTH, pairs)  41.1 us
    pallas_call x1, Pallas kernels, attend(): pl.pallas_call(attend_kernel, grid_spec=pltpu.PrefetchScalarGridSpec(num_...  14.4 us
    pallas_call x2, Pallas kernels, widen(): pl.pallas_call(widen_kernel, in_specs=[IN_VMEM] * (len(rows) + 2), out_sp...  8.28 us
    pallas_call x2, Pallas kernels, narrow(): pl.pallas_call(narrow_kernel, in_specs=[IN_VMEM] * 5, out_specs=[IN_VMEM]...  5.45 us
    pallas_call x2, Pallas kernels, mix(): pl.pallas_call(functools.partial(mix_kernel, half, by_inner), in_specs=[I...  4.66 us
    ppermute x5, waiting for transfers between devices, swap_cores(): return lax.ppermute(value, 'narrow', [(0, 1), (1, 0)])  4.03 us
  transfers between devices with their start and end apart: 36, of which 19 were waited for; matrix products, arithmetic and copies ran while one was open for 0% of the time, Pallas kernels for 19%

profile of v1, /device:TPU:0, one launch (start us, length us, event | category | flops | bytes accessed | tf_op | source)
XLA Modules:
  0.0 180.1 jit_solution(9961294215443783043)
XLA Ops:
  0.7 2.8 %pack.1 = (bf16[32,3712]{1,0:T(8,128)(2,1)}, bf16[576,256]{1,0:T(8,128)(2,1)}) custom-call(s32[2,8]{1,0:T(2,128)} %bitcast.6, bf16[4,8,3584]{2,1,0:T(8,128)(2,1)} %token_hbm.1, s32[4,8,8]{2,1,0:T(8,128)} %id_hbm.1, f32[4,8,8]{2,1,0:T(8,128)} %affinity_hbm.1, bf16[8,576,1024]{2,1,0:T(8,128)(2,1)} %bitcast.4), custom_call_target="tpu_custom_call" | custom-call | flops 330000000 | bytes 1 | tf_op jit(solution)/shard_map/pack/pallas_call | solution.py:233
  6.6 2.7 %collective-permute-start.2 = (bf16[32,3712]{1,0:T(8,128)(2,1)}, bf16[32,3712]{1,0:T(8,128)(2,1)S(1)}, u32[]{:S(2)}, u32[]{:S(2)}) collective-permute-start(bf16[32,3712]{1,0:T(8,128)(2,1)} %get-tuple-element.61.refs_0_), channel_id=1, source_target_pairs={{0,4},{1,5},{2,6},{3,7},{4,0},{5,1},{6,2},{7,3},{8,12},{9,13},{10,... | collective-permute-start | bytes 712712 | tf_op jit(solution)/shard_map/ppermute | solution.py:52
  10.4 10.5 %collective-permute-done.1.refs_1_ = bf16[32,3712]{1,0:T(8,128)(2,1)S(1)} collective-permute-done((bf16[32,3712]{1,0:T(8,128)(2,1)}, bf16[32,3712]{1,0:T(8,128)(2,1)S(1)}, u32[]{:S(2)}, u32[]{:S(2)}) %collective-permute-start.1) | collective-permute-done | bytes 237600 | tf_op jit(solution)/shard_map/ppermute | solution.py:52
  21.0 4.3 %collective-permute-done.2.refs_2_ = bf16[32,3712]{1,0:T(8,128)(2,1)S(1)} collective-permute-done((bf16[32,3712]{1,0:T(8,128)(2,1)}, bf16[32,3712]{1,0:T(8,128)(2,1)S(1)}, u32[]{:S(2)}, u32[]{:S(2)}) %collective-permute-start.2) | collective-permute-done | bytes 237600 | tf_op jit(solution)/shard_map/ppermute | solution.py:52
  27.9 2.9 %collective-permute-start.6 = (bf16[128,3712]{1,0:T(8,128)(2,1)S(1)}, bf16[128,3712]{1,0:T(8,128)(2,1)S(1)}, u32[]{:S(2)}, u32[]{:S(2)}) collective-permute-start(bf16[128,3712]{1,0:T(8,128)(2,1)S(1)} %stack.1.refs_0_), channel_id=1, source_target_pairs={{0,16},{1,65},{2,18},{3,67},{4,20},{5,69},{6,22},{7,71},{8,24},{9,... | collective-permute-start | bytes 2850824 | tf_op jit(solution)/shard_map/ppermute | solution.py:52
  33.5 14.4 %attend.1 = bf16[4,8,64,512]{3,2,1,0:T(8,128)(2,1)} custom-call(s32[8]{0:T(128)S(1)} %copy-done.6, s32[2,8]{1,0:T(2,128)S(1)} %bitcast.3, bf16[4,8,64,576]{3,2,1,0:T(8,128)(2,1)} %query_hbm.1, bf16[8,576,1024]{2,1,0:T(8,128)(2,1)} %bitcast.5, bf16[576,256]{1,0:T(8,128)(2,1)S(1)} %collective-permute-done.moved_ref, ...), custom_call_target="tpu_custom_call" | custom-call | flops 1320000000 | bytes 1 | tf_op jit(solution)/shard_map/attend/pallas_call | solution.py:168
  47.9 4.9 %collective-permute-done.6.refs_2_ = bf16[128,3712]{1,0:T(8,128)(2,1)S(1)} collective-permute-done((bf16[128,3712]{1,0:T(8,128)(2,1)S(1)}, bf16[128,3712]{1,0:T(8,128)(2,1)S(1)}, u32[]{:S(2)}, u32[]{:S(2)}) %collective-permute-start.6) | collective-permute-done | bytes 950304 | tf_op jit(solution)/shard_map/ppermute | solution.py:52
  54.1 2.0 %collective-permute-start.8 = (bf16[128,3584]{1,0:T(8,128)(2,1)S(1)}, bf16[128,3584]{1,0:T(8,128)(2,1)S(1)}, u32[]{:S(2)}, u32[]{:S(2)}) collective-permute-start(bf16[128,3584]{1,0:T(8,128)(2,1)S(1)} %get-tuple-element.71), channel_id=1, source_target_pairs={{0,32},{1,9},{2,34},{3,11},{4,36},{5,13},{6,38},{7,15},{8,40},{9,1... | collective-permute-start | bytes 2752520 | tf_op jit(solution)/shard_map/ppermute | solution.py:52
  56.1 3.2 %collective-permute-start.9 = (bf16[128,3584]{1,0:T(8,128)(2,1)S(1)}, bf16[128,3584]{1,0:T(8,128)(2,1)S(1)}, u32[]{:S(2)}, u32[]{:S(2)}) collective-permute-start(bf16[128,3584]{1,0:T(8,128)(2,1)S(1)} %get-tuple-element.72), channel_id=1, source_target_pairs={{0,64},{1,17},{2,66},{3,19},{4,68},{5,21},{6,70},{7,23},{8,72},{9,... | collective-permute-start | bytes 2752520 | tf_op jit(solution)/shard_map/ppermute | solution.py:52
  63.2 6.0 %collective-permute-done.8.refs_1_ = bf16[128,3584]{1,0:T(8,128)(2,1)S(1)} collective-permute-done((bf16[128,3584]{1,0:T(8,128)(2,1)S(1)}, bf16[128,3584]{1,0:T(8,128)(2,1)S(1)}, u32[]{:S(2)}, u32[]{:S(2)}) %collective-permute-start.8) | collective-permute-done | bytes 917536 | tf_op jit(solution)/shard_map/ppermute | solution.py:52
  69.2 2.0 %collective-permute-start.15 = (bf16[128,3584]{1,0:T(8,128)(2,1)S(1)}, bf16[128,3584]{1,0:T(8,128)(2,1)S(1)}, u32[]{:S(2)}, u32[]{:S(2)}) collective-permute-start(bf16[128,3584]{1,0:T(8,128)(2,1)S(1)} %get-tuple-element.85), channel_id=1, source_target_pairs={{0,96},{1,25},{2,98},{3,27},{4,100},{5,29},{6,102},{7,31},{8,104},... | collective-permute-start | bytes 2752520 | tf_op jit(solution)/shard_map/ppermute | solution.py:52
  71.2 9.4 %collective-permute-done.9.refs_2_ = bf16[128,3584]{1,0:T(8,128)(2,1)S(1)} collective-permute-done((bf16[128,3584]{1,0:T(8,128)(2,1)S(1)}, bf16[128,3584]{1,0:T(8,128)(2,1)S(1)}, u32[]{:S(2)}, u32[]{:S(2)}) %collective-permute-start.9) | collective-permute-done | bytes 917536 | tf_op jit(solution)/shard_map/ppermute | solution.py:52
  80.6 4.1 %widen.2 = (f32[512,512]{1,0:T(8,128)S(1)}, f32[512,512]{1,0:T(8,128)S(1)}, bf16[512,512]{1,0:T(8,128)(2,1)S(1)}, bf16[512,512]{1,0:T(8,128)(2,1)S(1)}) custom-call(bf16[128,3584]{1,0:T(8,128)(2,1)S(1)} %get-tuple-element.70.refs_0_, bf16[128,3584]{1,0:T(8,128)(2,1)S(1)} %collective-permute-done.8.refs_1_, ...), custom_call_target="tpu_custom_call" | custom-call | flops 550000000 | bytes 1 | tf_op jit(solution)/shard_map/widen/pallas_call | solution.py:410
  87.5 2.7 %narrow.2 = (bf16[128,3584]{1,0:T(8,128)(2,1)S(1)}, bf16[128,3584]{1,0:T(8,128)(2,1)S(1)}, bf16[128,3584]{1,0:T(8,128)(2,1)S(1)}, bf16[128,3584]{1,0:T(8,128)(2,1)S(1)}) custom-call(f32[512,512]{1,0:T(8,128)S(1)} %get-tuple-element.74.gate_own, f32[512,512]{1,0:T(8,128)S(1)} %get-tuple-element.75.up_own, ...), custom_call_target="tpu_custom_call" | custom-call | flops 330000000 | bytes 1 | tf_op jit(solution)/shard_map/narrow/pallas_call | solution.py:457
  90.3 9.9 %collective-permute-done.14.refs_2_ = bf16[128,3584]{1,0:T(8,128)(2,1)S(1)} collective-permute-done((bf16[128,3584]{1,0:T(8,128)(2,1)S(1)}, bf16[128,3584]{1,0:T(8,128)(2,1)S(1)}, u32[]{:S(2)}, u32[]{:S(2)}) %collective-permute-start.14) | collective-permute-done | bytes 917536 | tf_op jit(solution)/shard_map/ppermute | solution.py:52
  100.2 2.1 %collective-permute-start.16 = (bf16[128,3584]{1,0:T(8,128)(2,1)S(1)}, bf16[128,3584]{1,0:T(8,128)(2,1)S(1)}, u32[]{:S(2)}, u32[]{:S(2)}) collective-permute-start(bf16[128,3584]{1,0:T(8,128)(2,1)S(1)} %get-tuple-element.87), channel_id=1, source_target_pairs={{0,96},{1,25},{2,98},{3,27},{4,100},{5,29},{6,102},{7,31},{8,104},... | collective-permute-start | bytes 2752520 | tf_op jit(solution)/shard_map/ppermute | solution.py:52
  102.3 4.1 %widen.3 = (f32[512,512]{1,0:T(8,128)S(1)}, f32[512,512]{1,0:T(8,128)S(1)}, bf16[512,512]{1,0:T(8,128)(2,1)S(1)}, bf16[512,512]{1,0:T(8,128)(2,1)S(1)}) custom-call(bf16[128,3584]{1,0:T(8,128)(2,1)S(1)} %get-tuple-element.98.refs_0_, bf16[128,3584]{1,0:T(8,128)(2,1)S(1)} %collective-permute-done.13.refs_1_, ...), custom_call_target="tpu_custom_call" | custom-call | flops 550000000 | bytes 1 | tf_op jit(solution)/shard_map/widen/pallas_call | solution.py:410
  107.1 1.8 %collective-permute-start.17 = (bf16[128,3584]{1,0:T(8,128)(2,1)S(1)}, bf16[128,3584]{1,0:T(8,128)(2,1)S(1)}, u32[]{:S(2)}, u32[]{:S(2)}) collective-permute-start(bf16[128,3584]{1,0:T(8,128)(2,1)S(1)} %get-tuple-element.88), channel_id=1, source_target_pairs={{0,64},{1,17},{2,66},{3,19},{4,68},{5,21},{6,70},{7,23},{8,72},{9,... | collective-permute-start | bytes 2752520 | tf_op jit(solution)/shard_map/ppermute | solution.py:52
  109.2 2.7 %narrow.3 = (bf16[128,3584]{1,0:T(8,128)(2,1)S(1)}, bf16[128,3584]{1,0:T(8,128)(2,1)S(1)}, bf16[128,3584]{1,0:T(8,128)(2,1)S(1)}, bf16[128,3584]{1,0:T(8,128)(2,1)S(1)}) custom-call(f32[512,512]{1,0:T(8,128)S(1)} %get-tuple-element.102.gate_own, f32[512,512]{1,0:T(8,128)S(1)} %get-tuple-element.103.up_own, ...), custom_call_target="tpu_custom_call" | custom-call | flops 330000000 | bytes 1 | tf_op jit(solution)/shard_map/narrow/pallas_call | solution.py:457
  111.9 3.0 %collective-permute-start.27 = (bf16[128,3584]{1,0:T(8,128)(2,1)S(1)}, bf16[128,3584]{1,0:T(8,128)(2,1)S(1)}, u32[]{:S(2)}, u32[]{:S(2)}) collective-permute-start(bf16[128,3584]{1,0:T(8,128)(2,1)S(1)} %get-tuple-element.107), channel_id=1, source_target_pairs={{0,96},{1,25},{2,98},{3,27},{4,100},{5,29},{6,102},{7,31},{8,104},... | collective-permute-start | bytes 2752520 | tf_op jit(solution)/shard_map/ppermute | solution.py:52
  115.4 7.7 %collective-permute-done.16.refs_5_ = bf16[128,3584]{1,0:T(8,128)(2,1)S(1)} collective-permute-done((bf16[128,3584]{1,0:T(8,128)(2,1)S(1)}, bf16[128,3584]{1,0:T(8,128)(2,1)S(1)}, u32[]{:S(2)}, u32[]{:S(2)}) %collective-permute-start.16) | collective-permute-done | bytes 917536 | tf_op jit(solution)/shard_map/ppermute | solution.py:52
  123.1 8.7 %collective-permute-done.18.refs_7_ = bf16[128,3584]{1,0:T(8,128)(2,1)S(1)} collective-permute-done((bf16[128,3584]{1,0:T(8,128)(2,1)S(1)}, bf16[128,3584]{1,0:T(8,128)(2,1)S(1)}, u32[]{:S(2)}, u32[]{:S(2)}) %collective-permute-start.18) | collective-permute-done | bytes 917536 | tf_op jit(solution)/shard_map/ppermute | solution.py:52
  131.8 2.3 %mix.2 = (bf16[64,3584]{1,0:T(8,128)(2,1)S(1)}, bf16[64,3584]{1,0:T(8,128)(2,1)S(1)}, bf16[64,3584]{1,0:T(8,128)(2,1)S(1)}, bf16[64,3584]{1,0:T(8,128)(2,1)S(1)}) custom-call(bf16[128,3712]{1,0:T(8,128)(2,1)S(1)} %stack.1.refs_0_, bf16[128,3712]{1,0:T(8,128)(2,1)S(1)} %collective-permute-done.5.refs_1_, ...), custom_call_target="tpu_custom_call" | custom-call | flops 275000000 | bytes 1 | tf_op jit(solution)/shard_map/mix/pallas_call | solution.py:372
  134.2 1.7 collective-permute-start.20
  135.9 6.9 %collective-permute-done.27.refs_5_ = bf16[128,3584]{1,0:T(8,128)(2,1)S(1)} collective-permute-done((bf16[128,3584]{1,0:T(8,128)(2,1)S(1)}, bf16[128,3584]{1,0:T(8,128)(2,1)S(1)}, u32[]{:S(2)}, u32[]{:S(2)}) %collective-permute-start.27) | collective-permute-done | bytes 917536 | tf_op jit(solution)/shard_map/ppermute | solution.py:52
  142.8 8.7 %collective-permute-done.29.refs_7_ = bf16[128,3584]{1,0:T(8,128)(2,1)S(1)} collective-permute-done((bf16[128,3584]{1,0:T(8,128)(2,1)S(1)}, bf16[128,3584]{1,0:T(8,128)(2,1)S(1)}, u32[]{:S(2)}, u32[]{:S(2)}) %collective-permute-start.29) | collective-permute-done | bytes 917536 | tf_op jit(solution)/shard_map/ppermute | solution.py:52
  151.5 2.3 %mix.3 = (bf16[64,3584]{1,0:T(8,128)(2,1)S(1)}, bf16[64,3584]{1,0:T(8,128)(2,1)S(1)}, bf16[64,3584]{1,0:T(8,128)(2,1)S(1)}, bf16[64,3584]{1,0:T(8,128)(2,1)S(1)}) custom-call(bf16[128,3712]{1,0:T(8,128)(2,1)S(1)} %stack.1.refs_0_, bf16[128,3712]{1,0:T(8,128)(2,1)S(1)} %collective-permute-done.5.refs_1_, ...), custom_call_target="tpu_custom_call" | custom-call | flops 275000000 | bytes 1 | tf_op jit(solution)/shard_map/mix/pallas_call | solution.py:372
  153.8 2.7 %collective-permute-start.30 = (bf16[64,3584]{1,0:T(8,128)(2,1)S(1)}, bf16[64,3584]{1,0:T(8,128)(2,1)S(1)}, u32[]{:S(2)}, u32[]{:S(2)}) collective-permute-start(bf16[64,3584]{1,0:T(8,128)(2,1)S(1)} %get-tuple-element.111), channel_id=1, source_target_pairs={{0,24},{1,97},{2,26},{3,99},{4,28},{5,101},{6,30},{7,103},{8,0},{9... | collective-permute-start | bytes 1376264 | tf_op jit(solution)/shard_map/ppermute | solution.py:52
  158.4 3.0 %collective-permute-start.22 = (bf16[16,3584]{1,0:T(8,128)(2,1)S(1)}, bf16[16,3584]{1,0:T(8,128)(2,1)S(1)}, u32[]{:S(2)}, u32[]{:S(2)}) collective-permute-start(bf16[16,3584]{1,0:T(8,128)(2,1)S(1)} %get-tuple-element.95), channel_id=1, source_target_pairs={{0,24},{1,97},{2,26},{3,99},{4,28},{5,101},{6,30},{7,103},{8,0},{9... | collective-permute-start | bytes 344072 | tf_op jit(solution)/shard_map/ppermute | solution.py:52
  162.4 5.1 %collective-permute-done.30.refs_1_ = bf16[64,3584]{1,0:T(8,128)(2,1)S(1)} collective-permute-done((bf16[64,3584]{1,0:T(8,128)(2,1)S(1)}, bf16[64,3584]{1,0:T(8,128)(2,1)S(1)}, u32[]{:S(2)}, u32[]{:S(2)}) %collective-permute-start.30) | collective-permute-done | bytes 458784 | tf_op jit(solution)/shard_map/ppermute | solution.py:52
  167.4 3.9 %collective-permute-done.32.refs_3_ = bf16[64,3584]{1,0:T(8,128)(2,1)S(1)} collective-permute-done((bf16[64,3584]{1,0:T(8,128)(2,1)S(1)}, bf16[64,3584]{1,0:T(8,128)(2,1)S(1)}, u32[]{:S(2)}, u32[]{:S(2)}) %collective-permute-start.32) | collective-permute-done | bytes 458784 | tf_op jit(solution)/shard_map/ppermute | solution.py:52
  174.4 2.1 %collective-permute-done.33.refs_5_ = bf16[16,3584]{1,0:T(8,128)(2,1)S(1)} collective-permute-done((bf16[16,3584]{1,0:T(8,128)(2,1)S(1)}, bf16[16,3584]{1,0:T(8,128)(2,1)S(1)}, u32[]{:S(2)}, u32[]{:S(2)}) %collective-permute-start.33) | collective-permute-done | bytes 114720 | tf_op jit(solution)/shard_map/ppermute | solution.py:52
  (68 shorter events, 28.5 us)
Async XLA Ops:
  3.4 22.9 %collective-permute-start = (bf16[576,256]{1,0:T(8,128)(2,1)}, bf16[576,256]{1,0:T(8,128)(2,1)S(1)}, u32[]{:S(2)}, u32[]{:S(2)}) collective-permute-start(bf16[576,256]{1,0:T(8,128)(2,1)} %get-tuple-element.60), channel_id=1, source_target_pairs={{0,2},{1,5},{2,4},{3,7},{4,6},{5,9},{6,8},{7,11},{8,10},{9,13},{10... | collective-permute-start | bytes 884744 | tf_op jit(solution)/shard_map/ppermute | solution.py:559
  5.1 15.9 %collective-permute-start.1 = (bf16[32,3712]{1,0:T(8,128)(2,1)}, bf16[32,3712]{1,0:T(8,128)(2,1)S(1)}, u32[]{:S(2)}, u32[]{:S(2)}) collective-permute-start(bf16[32,3712]{1,0:T(8,128)(2,1)} %get-tuple-element.61.refs_0_), channel_id=1, source_target_pairs={{0,2},{1,3},{2,4},{3,5},{4,6},{5,7},{6,0},{7,1},{8,10},{9,11},{10,... | collective-permute-start | bytes 712712 | tf_op jit(solution)/shard_map/ppermute | solution.py:52
  6.6 18.7 %collective-permute-start.2 = (bf16[32,3712]{1,0:T(8,128)(2,1)}, bf16[32,3712]{1,0:T(8,128)(2,1)S(1)}, u32[]{:S(2)}, u32[]{:S(2)}) collective-permute-start(bf16[32,3712]{1,0:T(8,128)(2,1)} %get-tuple-element.61.refs_0_), channel_id=1, source_target_pairs={{0,4},{1,5},{2,6},{3,7},{4,0},{5,1},{6,2},{7,3},{8,12},{9,13},{10,... | collective-permute-start | bytes 712712 | tf_op jit(solution)/shard_map/ppermute | solution.py:52
  9.3 16.0 %collective-permute-start.3 = (bf16[32,3712]{1,0:T(8,128)(2,1)}, bf16[32,3712]{1,0:T(8,128)(2,1)S(1)}, u32[]{:S(2)}, u32[]{:S(2)}) collective-permute-start(bf16[32,3712]{1,0:T(8,128)(2,1)} %get-tuple-element.61.refs_0_), channel_id=1, source_target_pairs={{0,6},{1,7},{2,0},{3,1},{4,2},{5,3},{6,4},{7,5},{8,14},{9,15},{10,... | collective-permute-start | bytes 712712 | tf_op jit(solution)/shard_map/ppermute | solution.py:52
  26.3 21.6 %collective-permute-start.5 = (bf16[128,3712]{1,0:T(8,128)(2,1)S(1)}, bf16[128,3712]{1,0:T(8,128)(2,1)S(1)}, u32[]{:S(2)}, u32[]{:S(2)}) collective-permute-start(bf16[128,3712]{1,0:T(8,128)(2,1)S(1)} %stack.1.refs_0_), channel_id=1, source_target_pairs={{0,8},{1,33},{2,10},{3,35},{4,12},{5,37},{6,14},{7,39},{8,16},{9,4... | collective-permute-start | bytes 2850824 | tf_op jit(solution)/shard_map/ppermute | solution.py:52
  27.9 24.8 %collective-permute-start.6 = (bf16[128,3712]{1,0:T(8,128)(2,1)S(1)}, bf16[128,3712]{1,0:T(8,128)(2,1)S(1)}, u32[]{:S(2)}, u32[]{:S(2)}) collective-permute-start(bf16[128,3712]{1,0:T(8,128)(2,1)S(1)} %stack.1.refs_0_), channel_id=1, source_target_pairs={{0,16},{1,65},{2,18},{3,67},{4,20},{5,69},{6,22},{7,71},{8,24},{9,... | collective-permute-start | bytes 2850824 | tf_op jit(solution)/shard_map/ppermute | solution.py:52
  30.8 21.9 %collective-permute-start.7 = (bf16[128,3712]{1,0:T(8,128)(2,1)S(1)}, bf16[128,3712]{1,0:T(8,128)(2,1)S(1)}, u32[]{:S(2)}, u32[]{:S(2)}) collective-permute-start(bf16[128,3712]{1,0:T(8,128)(2,1)S(1)} %stack.1.refs_0_), channel_id=1, source_target_pairs={{0,24},{1,97},{2,26},{3,99},{4,28},{5,101},{6,30},{7,103},{8,0},{9... | collective-permute-start | bytes 2850824 | tf_op jit(solution)/shard_map/ppermute | solution.py:52
  54.1 15.1 %collective-permute-start.8 = (bf16[128,3584]{1,0:T(8,128)(2,1)S(1)}, bf16[128,3584]{1,0:T(8,128)(2,1)S(1)}, u32[]{:S(2)}, u32[]{:S(2)}) collective-permute-start(bf16[128,3584]{1,0:T(8,128)(2,1)S(1)} %get-tuple-element.71), channel_id=1, source_target_pairs={{0,32},{1,9},{2,34},{3,11},{4,36},{5,13},{6,38},{7,15},{8,40},{9,1... | collective-permute-start | bytes 2752520 | tf_op jit(solution)/shard_map/ppermute | solution.py:52
  56.1 24.6 %collective-permute-start.9 = (bf16[128,3584]{1,0:T(8,128)(2,1)S(1)}, bf16[128,3584]{1,0:T(8,128)(2,1)S(1)}, u32[]{:S(2)}, u32[]{:S(2)}) collective-permute-start(bf16[128,3584]{1,0:T(8,128)(2,1)S(1)} %get-tuple-element.72), channel_id=1, source_target_pairs={{0,64},{1,17},{2,66},{3,19},{4,68},{5,21},{6,70},{7,23},{8,72},{9,... | collective-permute-start | bytes 2752520 | tf_op jit(solution)/shard_map/ppermute | solution.py:52
  59.3 21.3 %collective-permute-start.10 = (bf16[128,3584]{1,0:T(8,128)(2,1)S(1)}, bf16[128,3584]{1,0:T(8,128)(2,1)S(1)}, u32[]{:S(2)}, u32[]{:S(2)}) collective-permute-start(bf16[128,3584]{1,0:T(8,128)(2,1)S(1)} %get-tuple-element.73), channel_id=1, source_target_pairs={{0,96},{1,25},{2,98},{3,27},{4,100},{5,29},{6,102},{7,31},{8,104},... | collective-permute-start | bytes 2752520 | tf_op jit(solution)/shard_map/ppermute | solution.py:52
  61.7 28.6 %collective-permute-start.13 = (bf16[128,3584]{1,0:T(8,128)(2,1)S(1)}, bf16[128,3584]{1,0:T(8,128)(2,1)S(1)}, u32[]{:S(2)}, u32[]{:S(2)}) collective-permute-start(bf16[128,3584]{1,0:T(8,128)(2,1)S(1)} %get-tuple-element.83), channel_id=1, source_target_pairs={{0,32},{1,9},{2,34},{3,11},{4,36},{5,13},{6,38},{7,15},{8,40},{9,1... | collective-permute-start | bytes 2752520 | tf_op jit(solution)/shard_map/ppermute | solution.py:52
  62.7 37.5 %collective-permute-start.14 = (bf16[128,3584]{1,0:T(8,128)(2,1)S(1)}, bf16[128,3584]{1,0:T(8,128)(2,1)S(1)}, u32[]{:S(2)}, u32[]{:S(2)}) collective-permute-start(bf16[128,3584]{1,0:T(8,128)(2,1)S(1)} %get-tuple-element.84), channel_id=1, source_target_pairs={{0,64},{1,17},{2,66},{3,19},{4,68},{5,21},{6,70},{7,23},{8,72},{9,... | collective-permute-start | bytes 2752520 | tf_op jit(solution)/shard_map/ppermute | solution.py:52
  69.2 31.0 %collective-permute-start.15 = (bf16[128,3584]{1,0:T(8,128)(2,1)S(1)}, bf16[128,3584]{1,0:T(8,128)(2,1)S(1)}, u32[]{:S(2)}, u32[]{:S(2)}) collective-permute-start(bf16[128,3584]{1,0:T(8,128)(2,1)S(1)} %get-tuple-element.85), channel_id=1, source_target_pairs={{0,96},{1,25},{2,98},{3,27},{4,100},{5,29},{6,102},{7,31},{8,104},... | collective-permute-start | bytes 2752520 | tf_op jit(solution)/shard_map/ppermute | solution.py:52
  84.9 2.6 %collective-permute-start.12 = (bf16[512,512]{1,0:T(8,128)(2,1)S(1)}, bf16[512,512]{1,0:T(8,128)(2,1)S(1)}, u32[]{:S(2)}, u32[]{:S(2)}) collective-permute-start(bf16[512,512]{1,0:T(8,128)(2,1)S(1)} %get-tuple-element.77), channel_id=1, source_target_pairs={{0,1},{1,0},{2,3},{3,2},{4,5},{5,4},{6,7},{7,6},{8,9},{9,8},{10,11... | collective-permute-start | bytes 1572872 | tf_op jit(solution)/shard_map/ppermute | solution.py:473
  100.2 22.9 %collective-permute-start.16 = (bf16[128,3584]{1,0:T(8,128)(2,1)S(1)}, bf16[128,3584]{1,0:T(8,128)(2,1)S(1)}, u32[]{:S(2)}, u32[]{:S(2)}) collective-permute-start(bf16[128,3584]{1,0:T(8,128)(2,1)S(1)} %get-tuple-element.87), channel_id=1, source_target_pairs={{0,96},{1,25},{2,98},{3,27},{4,100},{5,29},{6,102},{7,31},{8,104},... | collective-permute-start | bytes 2752520 | tf_op jit(solution)/shard_map/ppermute | solution.py:52
  107.1 16.0 %collective-permute-start.17 = (bf16[128,3584]{1,0:T(8,128)(2,1)S(1)}, bf16[128,3584]{1,0:T(8,128)(2,1)S(1)}, u32[]{:S(2)}, u32[]{:S(2)}) collective-permute-start(bf16[128,3584]{1,0:T(8,128)(2,1)S(1)} %get-tuple-element.88), channel_id=1, source_target_pairs={{0,64},{1,17},{2,66},{3,19},{4,68},{5,21},{6,70},{7,23},{8,72},{9,... | collective-permute-start | bytes 2752520 | tf_op jit(solution)/shard_map/ppermute | solution.py:52
  108.9 22.9 %collective-permute-start.18 = (bf16[128,3584]{1,0:T(8,128)(2,1)S(1)}, bf16[128,3584]{1,0:T(8,128)(2,1)S(1)}, u32[]{:S(2)}, u32[]{:S(2)}) collective-permute-start(bf16[128,3584]{1,0:T(8,128)(2,1)S(1)} %get-tuple-element.89), channel_id=1, source_target_pairs={{0,32},{1,9},{2,34},{3,11},{4,36},{5,13},{6,38},{7,15},{8,40},{9,1... | collective-permute-start | bytes 2752520 | tf_op jit(solution)/shard_map/ppermute | solution.py:52
  111.9 30.8 %collective-permute-start.27 = (bf16[128,3584]{1,0:T(8,128)(2,1)S(1)}, bf16[128,3584]{1,0:T(8,128)(2,1)S(1)}, u32[]{:S(2)}, u32[]{:S(2)}) collective-permute-start(bf16[128,3584]{1,0:T(8,128)(2,1)S(1)} %get-tuple-element.107), channel_id=1, source_target_pairs={{0,96},{1,25},{2,98},{3,27},{4,100},{5,29},{6,102},{7,31},{8,104},... | collective-permute-start | bytes 2752520 | tf_op jit(solution)/shard_map/ppermute | solution.py:52
  114.9 27.8 %collective-permute-start.28 = (bf16[128,3584]{1,0:T(8,128)(2,1)S(1)}, bf16[128,3584]{1,0:T(8,128)(2,1)S(1)}, u32[]{:S(2)}, u32[]{:S(2)}) collective-permute-start(bf16[128,3584]{1,0:T(8,128)(2,1)S(1)} %get-tuple-element.108), channel_id=1, source_target_pairs={{0,64},{1,17},{2,66},{3,19},{4,68},{5,21},{6,70},{7,23},{8,72},{9,... | collective-permute-start | bytes 2752520 | tf_op jit(solution)/shard_map/ppermute | solution.py:52
  123.1 28.4 %collective-permute-start.29 = (bf16[128,3584]{1,0:T(8,128)(2,1)S(1)}, bf16[128,3584]{1,0:T(8,128)(2,1)S(1)}, u32[]{:S(2)}, u32[]{:S(2)}) collective-permute-start(bf16[128,3584]{1,0:T(8,128)(2,1)S(1)} %get-tuple-element.109), channel_id=1, source_target_pairs={{0,32},{1,9},{2,34},{3,11},{4,36},{5,13},{6,38},{7,15},{8,40},{9,1... | collective-permute-start | bytes 2752520 | tf_op jit(solution)/shard_map/ppermute | solution.py:52
  134.1 23.8 %collective-permute-start.19 = (bf16[64,3584]{1,0:T(8,128)(2,1)S(1)}, bf16[64,3584]{1,0:T(8,128)(2,1)S(1)}, u32[]{:S(2)}, u32[]{:S(2)}) collective-permute-start(bf16[64,3584]{1,0:T(8,128)(2,1)S(1)} %get-tuple-element.91), channel_id=1, source_target_pairs={{0,6},{1,7},{2,0},{3,1},{4,2},{5,3},{6,4},{7,5},{8,14},{9,15},{10,... | collective-permute-start | bytes 1376264 | tf_op jit(solution)/shard_map/ppermute | solution.py:52
  134.2 24.0 %collective-permute-start.20 = (bf16[64,3584]{1,0:T(8,128)(2,1)S(1)}, bf16[64,3584]{1,0:T(8,128)(2,1)S(1)}, u32[]{:S(2)}, u32[]{:S(2)}) collective-permute-start(bf16[64,3584]{1,0:T(8,128)(2,1)S(1)} %get-tuple-element.92), channel_id=1, source_target_pairs={{0,4},{1,5},{2,6},{3,7},{4,0},{5,1},{6,2},{7,3},{8,12},{9,13},{10,... | collective-permute-start | bytes 1376264 | tf_op jit(solution)/shard_map/ppermute | solution.py:52
  142.8 15.4 %collective-permute-start.21 = (bf16[64,3584]{1,0:T(8,128)(2,1)S(1)}, bf16[64,3584]{1,0:T(8,128)(2,1)S(1)}, u32[]{:S(2)}, u32[]{:S(2)}) collective-permute-start(bf16[64,3584]{1,0:T(8,128)(2,1)S(1)} %get-tuple-element.93), channel_id=1, source_target_pairs={{0,2},{1,3},{2,4},{3,5},{4,6},{5,7},{6,0},{7,1},{8,10},{9,11},{10,... | collective-permute-start | bytes 1376264 | tf_op jit(solution)/shard_map/ppermute | solution.py:52
  153.8 13.6 %collective-permute-start.30 = (bf16[64,3584]{1,0:T(8,128)(2,1)S(1)}, bf16[64,3584]{1,0:T(8,128)(2,1)S(1)}, u32[]{:S(2)}, u32[]{:S(2)}) collective-permute-start(bf16[64,3584]{1,0:T(8,128)(2,1)S(1)} %get-tuple-element.111), channel_id=1, source_target_pairs={{0,24},{1,97},{2,26},{3,99},{4,28},{5,101},{6,30},{7,103},{8,0},{9... | collective-permute-start | bytes 1376264 | tf_op jit(solution)/shard_map/ppermute | solution.py:52
  156.5 11.0 %collective-permute-start.31 = (bf16[64,3584]{1,0:T(8,128)(2,1)S(1)}, bf16[64,3584]{1,0:T(8,128)(2,1)S(1)}, u32[]{:S(2)}, u32[]{:S(2)}) collective-permute-start(bf16[64,3584]{1,0:T(8,128)(2,1)S(1)} %get-tuple-element.112), channel_id=1, source_target_pairs={{0,16},{1,65},{2,18},{3,67},{4,20},{5,69},{6,22},{7,71},{8,24},{9,... | collective-permute-start | bytes 1376264 | tf_op jit(solution)/shard_map/ppermute | solution.py:52
  157.9 13.5 %collective-permute-start.32 = (bf16[64,3584]{1,0:T(8,128)(2,1)S(1)}, bf16[64,3584]{1,0:T(8,128)(2,1)S(1)}, u32[]{:S(2)}, u32[]{:S(2)}) collective-permute-start(bf16[64,3584]{1,0:T(8,128)(2,1)S(1)} %get-tuple-element.113), channel_id=1, source_target_pairs={{0,8},{1,33},{2,10},{3,35},{4,12},{5,37},{6,14},{7,39},{8,16},{9,4... | collective-permute-start | bytes 1376264 | tf_op jit(solution)/shard_map/ppermute | solution.py:52
  158.4 14.7 %collective-permute-start.22 = (bf16[16,3584]{1,0:T(8,128)(2,1)S(1)}, bf16[16,3584]{1,0:T(8,128)(2,1)S(1)}, u32[]{:S(2)}, u32[]{:S(2)}) collective-permute-start(bf16[16,3584]{1,0:T(8,128)(2,1)S(1)} %get-tuple-element.95), channel_id=1, source_target_pairs={{0,24},{1,97},{2,26},{3,99},{4,28},{5,101},{6,30},{7,103},{8,0},{9... | collective-permute-start | bytes 344072 | tf_op jit(solution)/shard_map/ppermute | solution.py:52
  161.4 13.0 %collective-permute-start.23 = (bf16[16,3584]{1,0:T(8,128)(2,1)S(1)}, bf16[16,3584]{1,0:T(8,128)(2,1)S(1)}, u32[]{:S(2)}, u32[]{:S(2)}) collective-permute-start(bf16[16,3584]{1,0:T(8,128)(2,1)S(1)} %get-tuple-element.96), channel_id=1, source_target_pairs={{0,16},{1,65},{2,18},{3,67},{4,20},{5,69},{6,22},{7,71},{8,24},{9,... | collective-permute-start | bytes 344072 | tf_op jit(solution)/shard_map/ppermute | solution.py:52
  167.4 7.0 %collective-permute-start.24 = (bf16[16,3584]{1,0:T(8,128)(2,1)S(1)}, bf16[16,3584]{1,0:T(8,128)(2,1)S(1)}, u32[]{:S(2)}, u32[]{:S(2)}) collective-permute-start(bf16[16,3584]{1,0:T(8,128)(2,1)S(1)} %get-tuple-element.97), channel_id=1, source_target_pairs={{0,8},{1,33},{2,10},{3,35},{4,12},{5,37},{6,14},{7,39},{8,16},{9,4... | collective-permute-start | bytes 344072 | tf_op jit(solution)/shard_map/ppermute | solution.py:52
  171.6 4.9 %collective-permute-start.33 = (bf16[16,3584]{1,0:T(8,128)(2,1)S(1)}, bf16[16,3584]{1,0:T(8,128)(2,1)S(1)}, u32[]{:S(2)}, u32[]{:S(2)}) collective-permute-start(bf16[16,3584]{1,0:T(8,128)(2,1)S(1)} %get-tuple-element.115), channel_id=1, source_target_pairs={{0,6},{1,7},{2,0},{3,1},{4,2},{5,3},{6,4},{7,5},{8,14},{9,15},{10,... | collective-permute-start | bytes 344072 | tf_op jit(solution)/shard_map/ppermute | solution.py:52
  171.7 6.4 %collective-permute-start.34 = (bf16[16,3584]{1,0:T(8,128)(2,1)S(1)}, bf16[16,3584]{1,0:T(8,128)(2,1)S(1)}, u32[]{:S(2)}, u32[]{:S(2)}) collective-permute-start(bf16[16,3584]{1,0:T(8,128)(2,1)S(1)} %get-tuple-element.116), channel_id=1, source_target_pairs={{0,4},{1,5},{2,6},{3,7},{4,0},{5,1},{6,2},{7,3},{8,12},{9,13},{10,... | collective-permute-start | bytes 344072 | tf_op jit(solution)/shard_map/ppermute | solution.py:52
  173.1 6.2 %collective-permute-start.35 = (bf16[16,3584]{1,0:T(8,128)(2,1)S(1)}, bf16[16,3584]{1,0:T(8,128)(2,1)S(1)}, u32[]{:S(2)}, u32[]{:S(2)}) collective-permute-start(bf16[16,3584]{1,0:T(8,128)(2,1)S(1)} %get-tuple-element.117), channel_id=1, source_target_pairs={{0,2},{1,3},{2,4},{3,5},{4,6},{5,7},{6,0},{7,1},{8,10},{9,11},{10,... | collective-permute-start | bytes 344072 | tf_op jit(solution)/shard_map/ppermute | solution.py:52
  (11 other events, 180.5 us)

commit v2 on v1

--- a/solution.py
+++ b/solution.py
@@ -375,7 +375,7 @@
         out_specs=[IN_VMEM] * SIDE,
         out_shape=four(rows // SIDE, half_width),
         compiler_params=params(16),
-        cost_estimate=cost(2.5),
+        cost_estimate=cost(60),
         name="mix",
     )(*pieces, *answers)
 

time: 181 us -> 176 us (0.972)
  waiting for transfers between devices: 94.9 us -> 91.6 us
    ppermute x30, waiting for transfers between devices: 90.9 us -> 85.8 us  [hop(): return lax.ppermute(value, BOTH, pairs)]
    ppermute x5, waiting for transfers between devices: 4.03 us -> 5.88 us  [swap_cores(): return lax.ppermute(value, 'narrow', [(0, 1), (1, 0)])]
  transfers between devices with their start and end apart: 36 -> 36, of which waited for: 19 -> 20; matrix products, arithmetic and copies ran while one was open for 0% -> 0% of each run, Pallas kernels for 19% -> 19%
where the time goes in v2:
time: 176 us; the launch traced here: 175 us
  waiting for transfers between devices  91.6 us (52%)
  starting transfers between devices  44.2 us (25%)
  Pallas kernels  37.8 us (21%)
    ppermute x30, waiting for transfers between devices, hop(): return lax.ppermute(value, BOTH, pairs)  85.8 us
    ppermute x30, starting transfers between devices, hop(): return lax.ppermute(value, BOTH, pairs)  41.4 us
    pallas_call x1, Pallas kernels, attend(): pl.pallas_call(attend_kernel, grid_spec=pltpu.PrefetchScalarGridSpec(num_...  12.6 us
    pallas_call x2, Pallas kernels, widen(): pl.pallas_call(widen_kernel, in_specs=[IN_VMEM] * (len(rows) + 2), out_sp...  8.28 us
    ppermute x5, waiting for transfers between devices, swap_cores(): return lax.ppermute(value, 'narrow', [(0, 1), (1, 0)])  5.88 us
    pallas_call x2, Pallas kernels, narrow(): pl.pallas_call(narrow_kernel, in_specs=[IN_VMEM] * 5, out_specs=[IN_VMEM]...  5.45 us
    pallas_call x2, Pallas kernels, mix(): pl.pallas_call(functools.partial(mix_kernel, half, by_inner), in_specs=[I...  4.66 us
  transfers between devices with their start and end apart: 36, of which 20 were waited for; matrix products, arithmetic and copies ran while one was open for 0% of the time, Pallas kernels for 19%

profile of v2, /device:TPU:0, one launch (start us, length us, event | category | flops | bytes accessed | tf_op | source)
XLA Modules:
  0.0 175.4 jit_solution(5975620076990207304)
XLA Ops:
  0.7 2.8 %pack.1 = (bf16[32,3712]{1,0:T(8,128)(2,1)}, bf16[576,256]{1,0:T(8,128)(2,1)}) custom-call(s32[2,8]{1,0:T(2,128)} %bitcast.6, bf16[4,8,3584]{2,1,0:T(8,128)(2,1)} %token_hbm.1, s32[4,8,8]{2,1,0:T(8,128)} %id_hbm.1, f32[4,8,8]{2,1,0:T(8,128)} %affinity_hbm.1, bf16[8,576,1024]{2,1,0:T(8,128)(2,1)} %bitcast.4), custom_call_target="tpu_custom_call" | custom-call | flops 330000000 | bytes 1 | tf_op jit(solution)/shard_map/pack/pallas_call | solution.py:233
  6.6 2.7 %collective-permute-start.2 = (bf16[32,3712]{1,0:T(8,128)(2,1)}, bf16[32,3712]{1,0:T(8,128)(2,1)S(1)}, u32[]{:S(2)}, u32[]{:S(2)}) collective-permute-start(bf16[32,3712]{1,0:T(8,128)(2,1)} %get-tuple-element.61.refs_0_), channel_id=1, source_target_pairs={{0,4},{1,5},{2,6},{3,7},{4,0},{5,1},{6,2},{7,3},{8,12},{9,13},{10,... | collective-permute-start | bytes 712712 | tf_op jit(solution)/shard_map/ppermute | solution.py:52
  10.4 10.5 %collective-permute-done.1.refs_1_ = bf16[32,3712]{1,0:T(8,128)(2,1)S(1)} collective-permute-done((bf16[32,3712]{1,0:T(8,128)(2,1)}, bf16[32,3712]{1,0:T(8,128)(2,1)S(1)}, u32[]{:S(2)}, u32[]{:S(2)}) %collective-permute-start.1) | collective-permute-done | bytes 237600 | tf_op jit(solution)/shard_map/ppermute | solution.py:52
  21.0 4.3 %collective-permute-done.2.refs_2_ = bf16[32,3712]{1,0:T(8,128)(2,1)S(1)} collective-permute-done((bf16[32,3712]{1,0:T(8,128)(2,1)}, bf16[32,3712]{1,0:T(8,128)(2,1)S(1)}, u32[]{:S(2)}, u32[]{:S(2)}) %collective-permute-start.2) | collective-permute-done | bytes 237600 | tf_op jit(solution)/shard_map/ppermute | solution.py:52
  27.9 2.9 %collective-permute-start.6 = (bf16[128,3712]{1,0:T(8,128)(2,1)S(1)}, bf16[128,3712]{1,0:T(8,128)(2,1)S(1)}, u32[]{:S(2)}, u32[]{:S(2)}) collective-permute-start(bf16[128,3712]{1,0:T(8,128)(2,1)S(1)} %stack.1.refs_0_), channel_id=1, source_target_pairs={{0,16},{1,65},{2,18},{3,67},{4,20},{5,69},{6,22},{7,71},{8,24},{9,... | collective-permute-start | bytes 2850824 | tf_op jit(solution)/shard_map/ppermute | solution.py:52
  33.5 12.6 %attend.1 = bf16[4,8,64,512]{3,2,1,0:T(8,128)(2,1)} custom-call(s32[8]{0:T(128)S(1)} %copy-done.6, s32[2,8]{1,0:T(2,128)S(1)} %bitcast.3, bf16[4,8,64,576]{3,2,1,0:T(8,128)(2,1)} %query_hbm.1, bf16[8,576,1024]{2,1,0:T(8,128)(2,1)} %bitcast.5, bf16[576,256]{1,0:T(8,128)(2,1)S(1)} %collective-permute-done.moved_ref, ...), custom_call_target="tpu_custom_call" | custom-call | flops 1320000000 | bytes 1 | tf_op jit(solution)/shard_map/attend/pallas_call | solution.py:168
  46.1 6.6 %collective-permute-done.6.refs_2_ = bf16[128,3712]{1,0:T(8,128)(2,1)S(1)} collective-permute-done((bf16[128,3712]{1,0:T(8,128)(2,1)S(1)}, bf16[128,3712]{1,0:T(8,128)(2,1)S(1)}, u32[]{:S(2)}, u32[]{:S(2)}) %collective-permute-start.6) | collective-permute-done | bytes 950304 | tf_op jit(solution)/shard_map/ppermute | solution.py:52
  54.1 2.0 %collective-permute-start.8 = (bf16[128,3584]{1,0:T(8,128)(2,1)S(1)}, bf16[128,3584]{1,0:T(8,128)(2,1)S(1)}, u32[]{:S(2)}, u32[]{:S(2)}) collective-permute-start(bf16[128,3584]{1,0:T(8,128)(2,1)S(1)} %get-tuple-element.71), channel_id=1, source_target_pairs={{0,32},{1,9},{2,34},{3,11},{4,36},{5,13},{6,38},{7,15},{8,40},{9,1... | collective-permute-start | bytes 2752520 | tf_op jit(solution)/shard_map/ppermute | solution.py:52
  56.1 3.2 %collective-permute-start.9 = (bf16[128,3584]{1,0:T(8,128)(2,1)S(1)}, bf16[128,3584]{1,0:T(8,128)(2,1)S(1)}, u32[]{:S(2)}, u32[]{:S(2)}) collective-permute-start(bf16[128,3584]{1,0:T(8,128)(2,1)S(1)} %get-tuple-element.72), channel_id=1, source_target_pairs={{0,64},{1,17},{2,66},{3,19},{4,68},{5,21},{6,70},{7,23},{8,72},{9,... | collective-permute-start | bytes 2752520 | tf_op jit(solution)/shard_map/ppermute | solution.py:52
  63.2 6.0 %collective-permute-done.8.refs_1_ = bf16[128,3584]{1,0:T(8,128)(2,1)S(1)} collective-permute-done((bf16[128,3584]{1,0:T(8,128)(2,1)S(1)}, bf16[128,3584]{1,0:T(8,128)(2,1)S(1)}, u32[]{:S(2)}, u32[]{:S(2)}) %collective-permute-start.8) | collective-permute-done | bytes 917536 | tf_op jit(solution)/shard_map/ppermute | solution.py:52
  69.2 2.0 %collective-permute-start.15 = (bf16[128,3584]{1,0:T(8,128)(2,1)S(1)}, bf16[128,3584]{1,0:T(8,128)(2,1)S(1)}, u32[]{:S(2)}, u32[]{:S(2)}) collective-permute-start(bf16[128,3584]{1,0:T(8,128)(2,1)S(1)} %get-tuple-element.85), channel_id=1, source_target_pairs={{0,96},{1,25},{2,98},{3,27},{4,100},{5,29},{6,102},{7,31},{8,104},... | collective-permute-start | bytes 2752520 | tf_op jit(solution)/shard_map/ppermute | solution.py:52
  71.2 9.4 %collective-permute-done.9.refs_2_ = bf16[128,3584]{1,0:T(8,128)(2,1)S(1)} collective-permute-done((bf16[128,3584]{1,0:T(8,128)(2,1)S(1)}, bf16[128,3584]{1,0:T(8,128)(2,1)S(1)}, u32[]{:S(2)}, u32[]{:S(2)}) %collective-permute-start.9) | collective-permute-done | bytes 917536 | tf_op jit(solution)/shard_map/ppermute | solution.py:52
  80.6 4.1 %widen.2 = (f32[512,512]{1,0:T(8,128)S(1)}, f32[512,512]{1,0:T(8,128)S(1)}, bf16[512,512]{1,0:T(8,128)(2,1)S(1)}, bf16[512,512]{1,0:T(8,128)(2,1)S(1)}) custom-call(bf16[128,3584]{1,0:T(8,128)(2,1)S(1)} %get-tuple-element.70.refs_0_, bf16[128,3584]{1,0:T(8,128)(2,1)S(1)} %collective-permute-done.8.refs_1_, ...), custom_call_target="tpu_custom_call" | custom-call | flops 550000000 | bytes 1 | tf_op jit(solution)/shard_map/widen/pallas_call | solution.py:410
  87.5 2.7 %narrow.2 = (bf16[128,3584]{1,0:T(8,128)(2,1)S(1)}, bf16[128,3584]{1,0:T(8,128)(2,1)S(1)}, bf16[128,3584]{1,0:T(8,128)(2,1)S(1)}, bf16[128,3584]{1,0:T(8,128)(2,1)S(1)}) custom-call(f32[512,512]{1,0:T(8,128)S(1)} %get-tuple-element.74.gate_own, f32[512,512]{1,0:T(8,128)S(1)} %get-tuple-element.75.up_own, ...), custom_call_target="tpu_custom_call" | custom-call | flops 330000000 | bytes 1 | tf_op jit(solution)/shard_map/narrow/pallas_call | solution.py:457
  90.3 9.9 %collective-permute-done.14.refs_2_ = bf16[128,3584]{1,0:T(8,128)(2,1)S(1)} collective-permute-done((bf16[128,3584]{1,0:T(8,128)(2,1)S(1)}, bf16[128,3584]{1,0:T(8,128)(2,1)S(1)}, u32[]{:S(2)}, u32[]{:S(2)}) %collective-permute-start.14) | collective-permute-done | bytes 917536 | tf_op jit(solution)/shard_map/ppermute | solution.py:52
  100.2 2.1 %collective-permute-start.16 = (bf16[128,3584]{1,0:T(8,128)(2,1)S(1)}, bf16[128,3584]{1,0:T(8,128)(2,1)S(1)}, u32[]{:S(2)}, u32[]{:S(2)}) collective-permute-start(bf16[128,3584]{1,0:T(8,128)(2,1)S(1)} %get-tuple-element.87), channel_id=1, source_target_pairs={{0,96},{1,25},{2,98},{3,27},{4,100},{5,29},{6,102},{7,31},{8,104},... | collective-permute-start | bytes 2752520 | tf_op jit(solution)/shard_map/ppermute | solution.py:52
  102.3 1.8 %collective-permute-start.17 = (bf16[128,3584]{1,0:T(8,128)(2,1)S(1)}, bf16[128,3584]{1,0:T(8,128)(2,1)S(1)}, u32[]{:S(2)}, u32[]{:S(2)}) collective-permute-start(bf16[128,3584]{1,0:T(8,128)(2,1)S(1)} %get-tuple-element.88), channel_id=1, source_target_pairs={{0,64},{1,17},{2,66},{3,19},{4,68},{5,21},{6,70},{7,23},{8,72},{9,... | collective-permute-start | bytes 2752520 | tf_op jit(solution)/shard_map/ppermute | solution.py:52
  104.2 4.1 %widen.3 = (f32[512,512]{1,0:T(8,128)S(1)}, f32[512,512]{1,0:T(8,128)S(1)}, bf16[512,512]{1,0:T(8,128)(2,1)S(1)}, bf16[512,512]{1,0:T(8,128)(2,1)S(1)}) custom-call(bf16[128,3584]{1,0:T(8,128)(2,1)S(1)} %get-tuple-element.98.refs_0_, bf16[128,3584]{1,0:T(8,128)(2,1)S(1)} %collective-permute-done.13.refs_1_, ...), custom_call_target="tpu_custom_call" | custom-call | flops 550000000 | bytes 1 | tf_op jit(solution)/shard_map/widen/pallas_call | solution.py:410
  111.1 2.7 %narrow.3 = (bf16[128,3584]{1,0:T(8,128)(2,1)S(1)}, bf16[128,3584]{1,0:T(8,128)(2,1)S(1)}, bf16[128,3584]{1,0:T(8,128)(2,1)S(1)}, bf16[128,3584]{1,0:T(8,128)(2,1)S(1)}) custom-call(f32[512,512]{1,0:T(8,128)S(1)} %get-tuple-element.102.gate_own, f32[512,512]{1,0:T(8,128)S(1)} %get-tuple-element.103.up_own, ...), custom_call_target="tpu_custom_call" | custom-call | flops 330000000 | bytes 1 | tf_op jit(solution)/shard_map/narrow/pallas_call | solution.py:457
  113.8 3.3 %collective-permute-start.27 = (bf16[128,3584]{1,0:T(8,128)(2,1)S(1)}, bf16[128,3584]{1,0:T(8,128)(2,1)S(1)}, u32[]{:S(2)}, u32[]{:S(2)}) collective-permute-start(bf16[128,3584]{1,0:T(8,128)(2,1)S(1)} %get-tuple-element.107), channel_id=1, source_target_pairs={{0,96},{1,25},{2,98},{3,27},{4,100},{5,29},{6,102},{7,31},{8,104},... | collective-permute-start | bytes 2752520 | tf_op jit(solution)/shard_map/ppermute | solution.py:52
  117.6 5.5 %collective-permute-done.16.refs_5_ = bf16[128,3584]{1,0:T(8,128)(2,1)S(1)} collective-permute-done((bf16[128,3584]{1,0:T(8,128)(2,1)S(1)}, bf16[128,3584]{1,0:T(8,128)(2,1)S(1)}, u32[]{:S(2)}, u32[]{:S(2)}) %collective-permute-start.16) | collective-permute-done | bytes 917536 | tf_op jit(solution)/shard_map/ppermute | solution.py:52
  123.1 3.9 %collective-permute-done.18.refs_7_ = bf16[128,3584]{1,0:T(8,128)(2,1)S(1)} collective-permute-done((bf16[128,3584]{1,0:T(8,128)(2,1)S(1)}, bf16[128,3584]{1,0:T(8,128)(2,1)S(1)}, u32[]{:S(2)}, u32[]{:S(2)}) %collective-permute-start.18) | collective-permute-done | bytes 917536 | tf_op jit(solution)/shard_map/ppermute | solution.py:52
  127.1 2.3 %mix.2 = (bf16[64,3584]{1,0:T(8,128)(2,1)S(1)}, bf16[64,3584]{1,0:T(8,128)(2,1)S(1)}, bf16[64,3584]{1,0:T(8,128)(2,1)S(1)}, bf16[64,3584]{1,0:T(8,128)(2,1)S(1)}) custom-call(bf16[128,3712]{1,0:T(8,128)(2,1)S(1)} %stack.1.refs_0_, bf16[128,3712]{1,0:T(8,128)(2,1)S(1)} %collective-permute-done.5.refs_1_, ...), custom_call_target="tpu_custom_call" | custom-call | flops 6600000000 | bytes 1 | tf_op jit(solution)/shard_map/mix/pallas_call | solution.py:372
  129.5 1.7 collective-permute-start.20
  131.2 11.6 %collective-permute-done.27.refs_5_ = bf16[128,3584]{1,0:T(8,128)(2,1)S(1)} collective-permute-done((bf16[128,3584]{1,0:T(8,128)(2,1)S(1)}, bf16[128,3584]{1,0:T(8,128)(2,1)S(1)}, u32[]{:S(2)}, u32[]{:S(2)}) %collective-permute-start.27) | collective-permute-done | bytes 917536 | tf_op jit(solution)/shard_map/ppermute | solution.py:52
  142.8 4.0 %collective-permute-done.29.refs_7_ = bf16[128,3584]{1,0:T(8,128)(2,1)S(1)} collective-permute-done((bf16[128,3584]{1,0:T(8,128)(2,1)S(1)}, bf16[128,3584]{1,0:T(8,128)(2,1)S(1)}, u32[]{:S(2)}, u32[]{:S(2)}) %collective-permute-start.29) | collective-permute-done | bytes 917536 | tf_op jit(solution)/shard_map/ppermute | solution.py:52
  146.8 2.3 %mix.3 = (bf16[64,3584]{1,0:T(8,128)(2,1)S(1)}, bf16[64,3584]{1,0:T(8,128)(2,1)S(1)}, bf16[64,3584]{1,0:T(8,128)(2,1)S(1)}, bf16[64,3584]{1,0:T(8,128)(2,1)S(1)}) custom-call(bf16[128,3712]{1,0:T(8,128)(2,1)S(1)} %stack.1.refs_0_, bf16[128,3712]{1,0:T(8,128)(2,1)S(1)} %collective-permute-done.5.refs_1_, ...), custom_call_target="tpu_custom_call" | custom-call | flops 6600000000 | bytes 1 | tf_op jit(solution)/shard_map/mix/pallas_call | solution.py:372
  149.1 2.7 %collective-permute-start.30 = (bf16[64,3584]{1,0:T(8,128)(2,1)S(1)}, bf16[64,3584]{1,0:T(8,128)(2,1)S(1)}, u32[]{:S(2)}, u32[]{:S(2)}) collective-permute-start(bf16[64,3584]{1,0:T(8,128)(2,1)S(1)} %get-tuple-element.111), channel_id=1, source_target_pairs={{0,24},{1,97},{2,26},{3,99},{4,28},{5,101},{6,30},{7,103},{8,0},{9... | collective-permute-start | bytes 1376264 | tf_op jit(solution)/shard_map/ppermute | solution.py:52
  153.7 3.6 %collective-permute-start.22 = (bf16[16,3584]{1,0:T(8,128)(2,1)S(1)}, bf16[16,3584]{1,0:T(8,128)(2,1)S(1)}, u32[]{:S(2)}, u32[]{:S(2)}) collective-permute-start(bf16[16,3584]{1,0:T(8,128)(2,1)S(1)} %get-tuple-element.95), channel_id=1, source_target_pairs={{0,24},{1,97},{2,26},{3,99},{4,28},{5,101},{6,30},{7,103},{8,0},{9... | collective-permute-start | bytes 344072 | tf_op jit(solution)/shard_map/ppermute | solution.py:52
  157.7 5.1 %collective-permute-done.30.refs_1_ = bf16[64,3584]{1,0:T(8,128)(2,1)S(1)} collective-permute-done((bf16[64,3584]{1,0:T(8,128)(2,1)S(1)}, bf16[64,3584]{1,0:T(8,128)(2,1)S(1)}, u32[]{:S(2)}, u32[]{:S(2)}) %collective-permute-start.30) | collective-permute-done | bytes 458784 | tf_op jit(solution)/shard_map/ppermute | solution.py:52
  162.8 3.9 %collective-permute-done.32.refs_3_ = bf16[64,3584]{1,0:T(8,128)(2,1)S(1)} collective-permute-done((bf16[64,3584]{1,0:T(8,128)(2,1)S(1)}, bf16[64,3584]{1,0:T(8,128)(2,1)S(1)}, u32[]{:S(2)}, u32[]{:S(2)}) %collective-permute-start.32) | collective-permute-done | bytes 458784 | tf_op jit(solution)/shard_map/ppermute | solution.py:52
  169.7 2.1 %collective-permute-done.33.refs_5_ = bf16[16,3584]{1,0:T(8,128)(2,1)S(1)} collective-permute-done((bf16[16,3584]{1,0:T(8,128)(2,1)S(1)}, bf16[16,3584]{1,0:T(8,128)(2,1)S(1)}, u32[]{:S(2)}, u32[]{:S(2)}) %collective-permute-start.33) | collective-permute-done | bytes 114720 | tf_op jit(solution)/shard_map/ppermute | solution.py:52
  (68 shorter events, 29.7 us)
Async XLA Ops:
  3.4 22.9 %collective-permute-start = (bf16[576,256]{1,0:T(8,128)(2,1)}, bf16[576,256]{1,0:T(8,128)(2,1)S(1)}, u32[]{:S(2)}, u32[]{:S(2)}) collective-permute-start(bf16[576,256]{1,0:T(8,128)(2,1)} %get-tuple-element.60), channel_id=1, source_target_pairs={{0,2},{1,5},{2,4},{3,7},{4,6},{5,9},{6,8},{7,11},{8,10},{9,13},{10... | collective-permute-start | bytes 884744 | tf_op jit(solution)/shard_map/ppermute | solution.py:559
  5.1 15.9 %collective-permute-start.1 = (bf16[32,3712]{1,0:T(8,128)(2,1)}, bf16[32,3712]{1,0:T(8,128)(2,1)S(1)}, u32[]{:S(2)}, u32[]{:S(2)}) collective-permute-start(bf16[32,3712]{1,0:T(8,128)(2,1)} %get-tuple-element.61.refs_0_), channel_id=1, source_target_pairs={{0,2},{1,3},{2,4},{3,5},{4,6},{5,7},{6,0},{7,1},{8,10},{9,11},{10,... | collective-permute-start | bytes 712712 | tf_op jit(solution)/shard_map/ppermute | solution.py:52
  6.6 18.7 %collective-permute-start.2 = (bf16[32,3712]{1,0:T(8,128)(2,1)}, bf16[32,3712]{1,0:T(8,128)(2,1)S(1)}, u32[]{:S(2)}, u32[]{:S(2)}) collective-permute-start(bf16[32,3712]{1,0:T(8,128)(2,1)} %get-tuple-element.61.refs_0_), channel_id=1, source_target_pairs={{0,4},{1,5},{2,6},{3,7},{4,0},{5,1},{6,2},{7,3},{8,12},{9,13},{10,... | collective-permute-start | bytes 712712 | tf_op jit(solution)/shard_map/ppermute | solution.py:52
  9.3 16.0 %collective-permute-start.3 = (bf16[32,3712]{1,0:T(8,128)(2,1)}, bf16[32,3712]{1,0:T(8,128)(2,1)S(1)}, u32[]{:S(2)}, u32[]{:S(2)}) collective-permute-start(bf16[32,3712]{1,0:T(8,128)(2,1)} %get-tuple-element.61.refs_0_), channel_id=1, source_target_pairs={{0,6},{1,7},{2,0},{3,1},{4,2},{5,3},{6,4},{7,5},{8,14},{9,15},{10,... | collective-permute-start | bytes 712712 | tf_op jit(solution)/shard_map/ppermute | solution.py:52
  26.3 19.9 %collective-permute-start.5 = (bf16[128,3712]{1,0:T(8,128)(2,1)S(1)}, bf16[128,3712]{1,0:T(8,128)(2,1)S(1)}, u32[]{:S(2)}, u32[]{:S(2)}) collective-permute-start(bf16[128,3712]{1,0:T(8,128)(2,1)S(1)} %stack.1.refs_0_), channel_id=1, source_target_pairs={{0,8},{1,33},{2,10},{3,35},{4,12},{5,37},{6,14},{7,39},{8,16},{9,4... | collective-permute-start | bytes 2850824 | tf_op jit(solution)/shard_map/ppermute | solution.py:52
  27.9 24.8 %collective-permute-start.6 = (bf16[128,3712]{1,0:T(8,128)(2,1)S(1)}, bf16[128,3712]{1,0:T(8,128)(2,1)S(1)}, u32[]{:S(2)}, u32[]{:S(2)}) collective-permute-start(bf16[128,3712]{1,0:T(8,128)(2,1)S(1)} %stack.1.refs_0_), channel_id=1, source_target_pairs={{0,16},{1,65},{2,18},{3,67},{4,20},{5,69},{6,22},{7,71},{8,24},{9,... | collective-permute-start | bytes 2850824 | tf_op jit(solution)/shard_map/ppermute | solution.py:52
  30.8 21.9 %collective-permute-start.7 = (bf16[128,3712]{1,0:T(8,128)(2,1)S(1)}, bf16[128,3712]{1,0:T(8,128)(2,1)S(1)}, u32[]{:S(2)}, u32[]{:S(2)}) collective-permute-start(bf16[128,3712]{1,0:T(8,128)(2,1)S(1)} %stack.1.refs_0_), channel_id=1, source_target_pairs={{0,24},{1,97},{2,26},{3,99},{4,28},{5,101},{6,30},{7,103},{8,0},{9... | collective-permute-start | bytes 2850824 | tf_op jit(solution)/shard_map/ppermute | solution.py:52
  54.1 15.1 %collective-permute-start.8 = (bf16[128,3584]{1,0:T(8,128)(2,1)S(1)}, bf16[128,3584]{1,0:T(8,128)(2,1)S(1)}, u32[]{:S(2)}, u32[]{:S(2)}) collective-permute-start(bf16[128,3584]{1,0:T(8,128)(2,1)S(1)} %get-tuple-element.71), channel_id=1, source_target_pairs={{0,32},{1,9},{2,34},{3,11},{4,36},{5,13},{6,38},{7,15},{8,40},{9,1... | collective-permute-start | bytes 2752520 | tf_op jit(solution)/shard_map/ppermute | solution.py:52
  56.1 24.6 %collective-permute-start.9 = (bf16[128,3584]{1,0:T(8,128)(2,1)S(1)}, bf16[128,3584]{1,0:T(8,128)(2,1)S(1)}, u32[]{:S(2)}, u32[]{:S(2)}) collective-permute-start(bf16[128,3584]{1,0:T(8,128)(2,1)S(1)} %get-tuple-element.72), channel_id=1, source_target_pairs={{0,64},{1,17},{2,66},{3,19},{4,68},{5,21},{6,70},{7,23},{8,72},{9,... | collective-permute-start | bytes 2752520 | tf_op jit(solution)/shard_map/ppermute | solution.py:52
  59.3 21.3 %collective-permute-start.10 = (bf16[128,3584]{1,0:T(8,128)(2,1)S(1)}, bf16[128,3584]{1,0:T(8,128)(2,1)S(1)}, u32[]{:S(2)}, u32[]{:S(2)}) collective-permute-start(bf16[128,3584]{1,0:T(8,128)(2,1)S(1)} %get-tuple-element.73), channel_id=1, source_target_pairs={{0,96},{1,25},{2,98},{3,27},{4,100},{5,29},{6,102},{7,31},{8,104},... | collective-permute-start | bytes 2752520 | tf_op jit(solution)/shard_map/ppermute | solution.py:52
  61.7 28.6 %collective-permute-start.13 = (bf16[128,3584]{1,0:T(8,128)(2,1)S(1)}, bf16[128,3584]{1,0:T(8,128)(2,1)S(1)}, u32[]{:S(2)}, u32[]{:S(2)}) collective-permute-start(bf16[128,3584]{1,0:T(8,128)(2,1)S(1)} %get-tuple-element.83), channel_id=1, source_target_pairs={{0,32},{1,9},{2,34},{3,11},{4,36},{5,13},{6,38},{7,15},{8,40},{9,1... | collective-permute-start | bytes 2752520 | tf_op jit(solution)/shard_map/ppermute | solution.py:52
  62.7 37.5 %collective-permute-start.14 = (bf16[128,3584]{1,0:T(8,128)(2,1)S(1)}, bf16[128,3584]{1,0:T(8,128)(2,1)S(1)}, u32[]{:S(2)}, u32[]{:S(2)}) collective-permute-start(bf16[128,3584]{1,0:T(8,128)(2,1)S(1)} %get-tuple-element.84), channel_id=1, source_target_pairs={{0,64},{1,17},{2,66},{3,19},{4,68},{5,21},{6,70},{7,23},{8,72},{9,... | collective-permute-start | bytes 2752520 | tf_op jit(solution)/shard_map/ppermute | solution.py:52
  69.2 31.0 %collective-permute-start.15 = (bf16[128,3584]{1,0:T(8,128)(2,1)S(1)}, bf16[128,3584]{1,0:T(8,128)(2,1)S(1)}, u32[]{:S(2)}, u32[]{:S(2)}) collective-permute-start(bf16[128,3584]{1,0:T(8,128)(2,1)S(1)} %get-tuple-element.85), channel_id=1, source_target_pairs={{0,96},{1,25},{2,98},{3,27},{4,100},{5,29},{6,102},{7,31},{8,104},... | collective-permute-start | bytes 2752520 | tf_op jit(solution)/shard_map/ppermute | solution.py:52
  84.9 2.6 %collective-permute-start.12 = (bf16[512,512]{1,0:T(8,128)(2,1)S(1)}, bf16[512,512]{1,0:T(8,128)(2,1)S(1)}, u32[]{:S(2)}, u32[]{:S(2)}) collective-permute-start(bf16[512,512]{1,0:T(8,128)(2,1)S(1)} %get-tuple-element.77), channel_id=1, source_target_pairs={{0,1},{1,0},{2,3},{3,2},{4,5},{5,4},{6,7},{7,6},{8,9},{9,8},{10,11... | collective-permute-start | bytes 1572872 | tf_op jit(solution)/shard_map/ppermute | solution.py:473
  100.2 22.9 %collective-permute-start.16 = (bf16[128,3584]{1,0:T(8,128)(2,1)S(1)}, bf16[128,3584]{1,0:T(8,128)(2,1)S(1)}, u32[]{:S(2)}, u32[]{:S(2)}) collective-permute-start(bf16[128,3584]{1,0:T(8,128)(2,1)S(1)} %get-tuple-element.87), channel_id=1, source_target_pairs={{0,96},{1,25},{2,98},{3,27},{4,100},{5,29},{6,102},{7,31},{8,104},... | collective-permute-start | bytes 2752520 | tf_op jit(solution)/shard_map/ppermute | solution.py:52
  102.3 20.8 %collective-permute-start.17 = (bf16[128,3584]{1,0:T(8,128)(2,1)S(1)}, bf16[128,3584]{1,0:T(8,128)(2,1)S(1)}, u32[]{:S(2)}, u32[]{:S(2)}) collective-permute-start(bf16[128,3584]{1,0:T(8,128)(2,1)S(1)} %get-tuple-element.88), channel_id=1, source_target_pairs={{0,64},{1,17},{2,66},{3,19},{4,68},{5,21},{6,70},{7,23},{8,72},{9,... | collective-permute-start | bytes 2752520 | tf_op jit(solution)/shard_map/ppermute | solution.py:52
  104.2 22.9 %collective-permute-start.18 = (bf16[128,3584]{1,0:T(8,128)(2,1)S(1)}, bf16[128,3584]{1,0:T(8,128)(2,1)S(1)}, u32[]{:S(2)}, u32[]{:S(2)}) collective-permute-start(bf16[128,3584]{1,0:T(8,128)(2,1)S(1)} %get-tuple-element.89), channel_id=1, source_target_pairs={{0,32},{1,9},{2,34},{3,11},{4,36},{5,13},{6,38},{7,15},{8,40},{9,1... | collective-permute-start | bytes 2752520 | tf_op jit(solution)/shard_map/ppermute | solution.py:52
  113.8 29.0 %collective-permute-start.27 = (bf16[128,3584]{1,0:T(8,128)(2,1)S(1)}, bf16[128,3584]{1,0:T(8,128)(2,1)S(1)}, u32[]{:S(2)}, u32[]{:S(2)}) collective-permute-start(bf16[128,3584]{1,0:T(8,128)(2,1)S(1)} %get-tuple-element.107), channel_id=1, source_target_pairs={{0,96},{1,25},{2,98},{3,27},{4,100},{5,29},{6,102},{7,31},{8,104},... | collective-permute-start | bytes 2752520 | tf_op jit(solution)/shard_map/ppermute | solution.py:52
  117.1 25.7 %collective-permute-start.28 = (bf16[128,3584]{1,0:T(8,128)(2,1)S(1)}, bf16[128,3584]{1,0:T(8,128)(2,1)S(1)}, u32[]{:S(2)}, u32[]{:S(2)}) collective-permute-start(bf16[128,3584]{1,0:T(8,128)(2,1)S(1)} %get-tuple-element.108), channel_id=1, source_target_pairs={{0,64},{1,17},{2,66},{3,19},{4,68},{5,21},{6,70},{7,23},{8,72},{9,... | collective-permute-start | bytes 2752520 | tf_op jit(solution)/shard_map/ppermute | solution.py:52
  123.1 23.7 %collective-permute-start.29 = (bf16[128,3584]{1,0:T(8,128)(2,1)S(1)}, bf16[128,3584]{1,0:T(8,128)(2,1)S(1)}, u32[]{:S(2)}, u32[]{:S(2)}) collective-permute-start(bf16[128,3584]{1,0:T(8,128)(2,1)S(1)} %get-tuple-element.109), channel_id=1, source_target_pairs={{0,32},{1,9},{2,34},{3,11},{4,36},{5,13},{6,38},{7,15},{8,40},{9,1... | collective-permute-start | bytes 2752520 | tf_op jit(solution)/shard_map/ppermute | solution.py:52
  129.4 23.8 %collective-permute-start.19 = (bf16[64,3584]{1,0:T(8,128)(2,1)S(1)}, bf16[64,3584]{1,0:T(8,128)(2,1)S(1)}, u32[]{:S(2)}, u32[]{:S(2)}) collective-permute-start(bf16[64,3584]{1,0:T(8,128)(2,1)S(1)} %get-tuple-element.91), channel_id=1, source_target_pairs={{0,6},{1,7},{2,0},{3,1},{4,2},{5,3},{6,4},{7,5},{8,14},{9,15},{10,... | collective-permute-start | bytes 1376264 | tf_op jit(solution)/shard_map/ppermute | solution.py:52
  129.5 24.0 %collective-permute-start.20 = (bf16[64,3584]{1,0:T(8,128)(2,1)S(1)}, bf16[64,3584]{1,0:T(8,128)(2,1)S(1)}, u32[]{:S(2)}, u32[]{:S(2)}) collective-permute-start(bf16[64,3584]{1,0:T(8,128)(2,1)S(1)} %get-tuple-element.92), channel_id=1, source_target_pairs={{0,4},{1,5},{2,6},{3,7},{4,0},{5,1},{6,2},{7,3},{8,12},{9,13},{10,... | collective-permute-start | bytes 1376264 | tf_op jit(solution)/shard_map/ppermute | solution.py:52
  142.8 10.7 %collective-permute-start.21 = (bf16[64,3584]{1,0:T(8,128)(2,1)S(1)}, bf16[64,3584]{1,0:T(8,128)(2,1)S(1)}, u32[]{:S(2)}, u32[]{:S(2)}) collective-permute-start(bf16[64,3584]{1,0:T(8,128)(2,1)S(1)} %get-tuple-element.93), channel_id=1, source_target_pairs={{0,2},{1,3},{2,4},{3,5},{4,6},{5,7},{6,0},{7,1},{8,10},{9,11},{10,... | collective-permute-start | bytes 1376264 | tf_op jit(solution)/shard_map/ppermute | solution.py:52
  149.1 13.6 %collective-permute-start.30 = (bf16[64,3584]{1,0:T(8,128)(2,1)S(1)}, bf16[64,3584]{1,0:T(8,128)(2,1)S(1)}, u32[]{:S(2)}, u32[]{:S(2)}) collective-permute-start(bf16[64,3584]{1,0:T(8,128)(2,1)S(1)} %get-tuple-element.111), channel_id=1, source_target_pairs={{0,24},{1,97},{2,26},{3,99},{4,28},{5,101},{6,30},{7,103},{8,0},{9... | collective-permute-start | bytes 1376264 | tf_op jit(solution)/shard_map/ppermute | solution.py:52
  151.8 11.0 %collective-permute-start.31 = (bf16[64,3584]{1,0:T(8,128)(2,1)S(1)}, bf16[64,3584]{1,0:T(8,128)(2,1)S(1)}, u32[]{:S(2)}, u32[]{:S(2)}) collective-permute-start(bf16[64,3584]{1,0:T(8,128)(2,1)S(1)} %get-tuple-element.112), channel_id=1, source_target_pairs={{0,16},{1,65},{2,18},{3,67},{4,20},{5,69},{6,22},{7,71},{8,24},{9,... | collective-permute-start | bytes 1376264 | tf_op jit(solution)/shard_map/ppermute | solution.py:52
  153.2 13.5 %collective-permute-start.32 = (bf16[64,3584]{1,0:T(8,128)(2,1)S(1)}, bf16[64,3584]{1,0:T(8,128)(2,1)S(1)}, u32[]{:S(2)}, u32[]{:S(2)}) collective-permute-start(bf16[64,3584]{1,0:T(8,128)(2,1)S(1)} %get-tuple-element.113), channel_id=1, source_target_pairs={{0,8},{1,33},{2,10},{3,35},{4,12},{5,37},{6,14},{7,39},{8,16},{9,4... | collective-permute-start | bytes 1376264 | tf_op jit(solution)/shard_map/ppermute | solution.py:52
  153.7 14.7 %collective-permute-start.22 = (bf16[16,3584]{1,0:T(8,128)(2,1)S(1)}, bf16[16,3584]{1,0:T(8,128)(2,1)S(1)}, u32[]{:S(2)}, u32[]{:S(2)}) collective-permute-start(bf16[16,3584]{1,0:T(8,128)(2,1)S(1)} %get-tuple-element.95), channel_id=1, source_target_pairs={{0,24},{1,97},{2,26},{3,99},{4,28},{5,101},{6,30},{7,103},{8,0},{9... | collective-permute-start | bytes 344072 | tf_op jit(solution)/shard_map/ppermute | solution.py:52
  157.3 12.4 %collective-permute-start.23 = (bf16[16,3584]{1,0:T(8,128)(2,1)S(1)}, bf16[16,3584]{1,0:T(8,128)(2,1)S(1)}, u32[]{:S(2)}, u32[]{:S(2)}) collective-permute-start(bf16[16,3584]{1,0:T(8,128)(2,1)S(1)} %get-tuple-element.96), channel_id=1, source_target_pairs={{0,16},{1,65},{2,18},{3,67},{4,20},{5,69},{6,22},{7,71},{8,24},{9,... | collective-permute-start | bytes 344072 | tf_op jit(solution)/shard_map/ppermute | solution.py:52
  162.7 7.0 %collective-permute-start.24 = (bf16[16,3584]{1,0:T(8,128)(2,1)S(1)}, bf16[16,3584]{1,0:T(8,128)(2,1)S(1)}, u32[]{:S(2)}, u32[]{:S(2)}) collective-permute-start(bf16[16,3584]{1,0:T(8,128)(2,1)S(1)} %get-tuple-element.97), channel_id=1, source_target_pairs={{0,8},{1,33},{2,10},{3,35},{4,12},{5,37},{6,14},{7,39},{8,16},{9,4... | collective-permute-start | bytes 344072 | tf_op jit(solution)/shard_map/ppermute | solution.py:52
  166.9 4.9 %collective-permute-start.33 = (bf16[16,3584]{1,0:T(8,128)(2,1)S(1)}, bf16[16,3584]{1,0:T(8,128)(2,1)S(1)}, u32[]{:S(2)}, u32[]{:S(2)}) collective-permute-start(bf16[16,3584]{1,0:T(8,128)(2,1)S(1)} %get-tuple-element.115), channel_id=1, source_target_pairs={{0,6},{1,7},{2,0},{3,1},{4,2},{5,3},{6,4},{7,5},{8,14},{9,15},{10,... | collective-permute-start | bytes 344072 | tf_op jit(solution)/shard_map/ppermute | solution.py:52
  167.0 6.4 %collective-permute-start.34 = (bf16[16,3584]{1,0:T(8,128)(2,1)S(1)}, bf16[16,3584]{1,0:T(8,128)(2,1)S(1)}, u32[]{:S(2)}, u32[]{:S(2)}) collective-permute-start(bf16[16,3584]{1,0:T(8,128)(2,1)S(1)} %get-tuple-element.116), channel_id=1, source_target_pairs={{0,4},{1,5},{2,6},{3,7},{4,0},{5,1},{6,2},{7,3},{8,12},{9,13},{10,... | collective-permute-start | bytes 344072 | tf_op jit(solution)/shard_map/ppermute | solution.py:52
  168.4 6.2 %collective-permute-start.35 = (bf16[16,3584]{1,0:T(8,128)(2,1)S(1)}, bf16[16,3584]{1,0:T(8,128)(2,1)S(1)}, u32[]{:S(2)}, u32[]{:S(2)}) collective-permute-start(bf16[16,3584]{1,0:T(8,128)(2,1)S(1)} %get-tuple-element.117), channel_id=1, source_target_pairs={{0,2},{1,3},{2,4},{3,5},{4,6},{5,7},{6,0},{7,1},{8,10},{9,11},{10,... | collective-permute-start | bytes 344072 | tf_op jit(solution)/shard_map/ppermute | solution.py:52
  (11 other events, 183.5 us)
